TPU v7x, 32 devices: a whole 2x2x4 slice. The times are simulated.
32 devices in a mesh: tile: 16 (over z, x, core), loop: 2 (over y).
Axes of the slice: x: 2, y: 2, z: 4, core: 2. Of those that a mesh axis runs over, the one named last changes fastest.
Arguments:
- star_slot: int32 [16, 32, 128], P('tile', 'loop'), may hold values from 0 to 255
- star_block: int32 [16, 32], P('tile', 'loop'), may hold values from 0 to 1, as said below
- exposure: int32 [16, 32, 128], P('tile', 'loop'), may hold values from 0 to 511
- superpixel: int32 [16, 32, 128], P('tile', 'loop'), may hold values from 0 to 2047
- magnitude: float32 [16, 32, 128], P('tile', 'loop'), may hold values from -7 to 7
- weight: float32 [16, 32, 128], P('tile', 'loop'), may hold values from 0.25 to 4
Outputs:
- star_mags: float32 [16384], P(('tile', 'loop'))
- zero_points: float32 [1024], P('loop')
- flat_field: float32 [128, 256], P('tile')
Inputs may be any that keep to these rules, and one draw needn't show every extreme that they name: `star_block`: observation blocks of one device at positions 8 * o to 8 * o + 7 of its 16 blocks observe stars of the star shard held by loop index o of the same tile.
All inputs are finite; a program needn't handle non-finite values.
Results may differ from a plain program's by a relative error of at most 0.00022.
Values sent between devices are 32-bit elements; how exact they have to be, the bound alone decides.
A program may use at most 64 MiB of HBM per device.

v0:
```python
import jax
import jax.numpy as jnp
from jax import lax
from jax.sharding import PartitionSpec as P

FC = 256
ROWS_DEV = 8
SBLK_DEV = 2
EXP_DEV = 512
STAR_BLK = 256
ITERS = 2


SMOOTH = 2.0
RIDGE = 0.5


def extended(array, sides, width):
    for axis, dim in sides:
        peers, length = (lax.axis_size(axis), array.shape[dim])
        up = [(i, (i + 1) % peers) for i in range(peers - 1)]
        down = [(j, i) for i, j in up]
        last = lax.slice_in_dim(array, length - width, length, axis=dim)
        leading = lax.slice_in_dim(array, 0, width, axis=dim)
        before = lax.ppermute(last, axis, up)
        after = lax.ppermute(leading, axis, down)
        array = jnp.concatenate([before, array, after], axis=dim)
    return array


def scatter_add(values, targets, total):
    return jax.ops.segment_sum(values.reshape(-1), targets.reshape(-1), num_segments=total)


def combine(vector, other, factor):
    return jax.tree.map(lambda values, others: values + factor * others, vector, other)


def on_device(star_slot, star_block, exposure, superpixel, magnitude, weight):
    loop_size = lax.axis_size("loop")
    loop_rank = lax.axis_index("loop")
    tile_rank = lax.axis_index("tile")
    stars_dev = SBLK_DEV * STAR_BLK
    pixels = ROWS_DEV * FC
    star_local = (star_block[0][:, None] * STAR_BLK + star_slot[0]).reshape(loop_size, -1)
    expo_ids = exposure[0].reshape(loop_size, -1)
    pixel_ids = superpixel[0].reshape(loop_size, -1)
    weights = weight[0].reshape(loop_size, -1)
    magnitudes = magnitude[0].reshape(loop_size, -1)
    spread = star_local + lax.broadcasted_iota(jnp.int32, star_local.shape, 0) * stars_dev

    def exposure_total(parts):
        return lax.psum(parts, "tile")

    def flat_total(parts):
        return lax.psum(parts, "loop")

    weighted = weights * magnitudes
    rhs_stars, count_stars = (
        lax.psum_scatter(
            scatter_add(weighted, spread, loop_size * stars_dev),
            "loop",
            scatter_dimension=0,
            tiled=True,
        ),
        lax.psum_scatter(
            scatter_add(weights, spread, loop_size * stars_dev),
            "loop",
            scatter_dimension=0,
            tiled=True,
        ),
    )
    rhs_expo, count_expo = exposure_total(
        (scatter_add(weighted, expo_ids, EXP_DEV), scatter_add(weights, expo_ids, EXP_DEV))
    )
    rhs_flat, count_flat = flat_total(
        (scatter_add(weighted, pixel_ids, pixels), scatter_add(weights, pixel_ids, pixels))
    )
    right_side = (rhs_stars, rhs_expo, rhs_flat.reshape(ROWS_DEV, FC))
    diagonal = (
        count_stars + RIDGE,
        count_expo + RIDGE,
        count_flat.reshape(ROWS_DEV, FC) + (4.0 * SMOOTH + RIDGE),
    )

    def operate(vector):
        star_dir, expo_dir, flat_dir = vector
        flat_line = flat_dir.reshape(-1)
        piece = lax.all_gather(star_dir, "loop", axis=0, tiled=True)
        shard_count = piece.shape[0] // stars_dev
        nearby = star_local
        nearby = nearby + lax.broadcasted_iota(jnp.int32, nearby.shape, 0) * stars_dev
        weighted_fit = weights * (piece[nearby] + expo_dir[expo_ids] + flat_line[pixel_ids])
        partial_value = scatter_add(weighted_fit, nearby, shard_count * stars_dev)
        partial_value, expo_sum, flat_sum = (
            partial_value,
            scatter_add(weighted_fit, expo_ids, EXP_DEV),
            scatter_add(weighted_fit, pixel_ids, pixels),
        )
        star_sum = lax.psum_scatter(partial_value, "loop", scatter_dimension=0, tiled=True)
        (expo_sum,) = exposure_total((expo_sum,))
        (flat_sum,) = flat_total((flat_sum,))
        padded = extended(flat_dir, (("tile", 0),), 1)
        columns = jnp.pad(flat_dir, ((0, 0), (1, 1)))
        beside = padded[2:] + padded[:-2] + columns[:, 2:] + columns[:, :-2]
        return (
            star_sum + RIDGE * star_dir,
            expo_sum + RIDGE * expo_dir,
            flat_sum.reshape(ROWS_DEV, FC) + SMOOTH * (4.0 * flat_dir - beside) + RIDGE * flat_dir,
        )

    def inner_local(first_vec, second_vec):
        star_part = jnp.sum(first_vec[0] * second_vec[0])
        expo_part = jnp.where(tile_rank == 0, jnp.sum(first_vec[1] * second_vec[1]), 0.0)
        flat_part = jnp.where(loop_rank == 0, jnp.sum(first_vec[2] * second_vec[2]), 0.0)
        return star_part + expo_part + flat_part

    def divide(vector):
        return jax.tree.map(lambda values, scales: values / scales, vector, diagonal)

    solution = jax.tree.map(jnp.zeros_like, right_side)
    residual = right_side

    def paired(current, precon, image):
        return lax.psum(
            (inner_local(current, precon), inner_local(image, precon)), ("tile", "loop")
        )

    precon = divide(residual)
    image = operate(precon)
    norm_now, curvature = paired(residual, precon, image)
    step_size = norm_now / curvature
    direction, along = (precon, image)
    for iteration in range(ITERS):
        solution = combine(solution, direction, step_size)
        residual = combine(residual, along, -step_size)
        if iteration + 1 < ITERS:
            precon = divide(residual)
            image = operate(precon)
            norm_next, curvature = paired(residual, precon, image)
            ratio = norm_next / norm_now
            step_size = norm_next / (curvature - ratio * norm_next / step_size)
            direction = combine(precon, direction, ratio)
            along = combine(image, along, ratio)
            norm_now = norm_next
    return (solution[0], solution[1], solution[2])


def solution(mesh):
    in_specs = (
        P("tile", "loop", None),
        P("tile", "loop"),
        P("tile", "loop", None),
        P("tile", "loop", None),
        P("tile", "loop", None),
        P("tile", "loop", None),
    )
    out_specs = (P(("tile", "loop")), P("loop"), P("tile", None))
    return jax.shard_map(
        on_device, mesh=mesh, in_specs=in_specs, out_specs=out_specs, check_vma=False
    )
```

profile of v0, /device:TPU:0, one launch (start us, length us, event | category | flops | bytes accessed | tf_op | source)
XLA Modules:
  0.0 462.3 jit_solution(7202939463264359305)
XLA Ops:
  0.6 0.0 copy-start.5
  0.7 0.1 broadcast_bitcast_fusion
  0.7 0.0 copy-start
  0.7 0.6 copy-done.5
  1.3 0.1 mul.166
  1.4 0.0 copy-done
  1.4 0.0 copy-done.2
  1.4 0.1 add.277
  1.5 0.6 copy-done.1
  2.2 0.0 copy-start.3
  2.2 14.7 %scatter_custom_fusion.1 = f32[1024]{0:T(1024)S(1)} fusion(s32[2048]{0:T(1024)S(1)} %bitcast.58, f32[2048]{0:T(1024)S(1)} %bitcast.42, f32[]{:T(128)} %constant.12.clone.1), kind=kCustom, calls=%fused_computation.92 | custom fusion | flops 2048 | bytes 4100 | tf_op jit(solution)/shard_map/scatter-add | solution.py:32
  16.8 14.7 %scatter_custom_fusion = f32[1024]{0:T(1024)S(1)} fusion(s32[2048]{0:T(1024)S(1)} %bitcast.59, f32[2048]{0:T(1024)S(1)} %bitcast_multiply_fusion, f32[]{:T(128)} %constant.12.clone.1), kind=kCustom, calls=%fused_computation.94 | custom fusion | flops 2048 | bytes 4100 | tf_op jit(solution)/shard_map/scatter-add | solution.py:32
  31.5 0.0 copy-done.3
  31.5 11.4 %scatter_custom_fusion.4 = f32[2048]{0:T(1024)S(1)} fusion(s32[2048]{0:T(1024)S(1)} %bitcast.50, f32[2048]{0:T(1024)S(1)} %bitcast_multiply_fusion, f32[]{:T(128)} %constant.12.clone.1), kind=kCustom, calls=%fused_computation.67 | custom fusion | flops 2048 | bytes 8196 | tf_op jit(solution)/shard_map/scatter-add | solution.py:32
  43.0 11.4 %scatter_custom_fusion.5 = f32[2048]{0:T(1024)S(1)} fusion(s32[2048]{0:T(1024)S(1)} %bitcast.51, f32[2048]{0:T(1024)S(1)} %bitcast.43, f32[]{:T(128)} %constant.12.clone.1), kind=kCustom, calls=%fused_computation.65 | custom fusion | flops 2048 | bytes 8196 | tf_op jit(solution)/shard_map/scatter-add | solution.py:32
  54.4 9.7 %all-reduce.11 = (f32[1024]{0:T(1024)S(1)}, f32[1024]{0:T(1024)S(1)}, f32[2048]{0:T(1024)S(1)}, f32[2048]{0:T(1024)S(1)}) all-reduce(f32[1024]{0:T(1024)S(1)} %scatter_custom_fusion.1, f32[1024]{0:T(1024)S(1)} %scatter_custom_fusion, f32[2048]{0:T(1024)S(1)} %scatter_custom_fusion.4, ...), channel_id=3, replica_groups=mesh['tile'=16,'loop'=2] {'loop'}, use_global_device_ids=true, to_apply=%region_3.0.clone | all-reduce | flops 6144 | bytes 49152
  64.1 0.6 multiply_reduce_fusion.2
  64.7 0.0 copy-start.4
  64.7 1.3 collective-permute-start.1
  66.0 1.3 collective-permute-start
  67.3 0.0 copy-done.4
  67.4 14.7 %scatter_custom_fusion.2 = f32[512]{0:T(512)S(1)} fusion(s32[2048]{0:T(1024)S(1)} %bitcast.54, f32[2048]{0:T(1024)S(1)} %bitcast_multiply_fusion, f32[]{:T(128)} %constant.12.clone.1), kind=kCustom, calls=%fused_computation.106 | custom fusion | flops 2048 | bytes 2052 | tf_op jit(solution)/shard_map/scatter-add | solution.py:32
  82.0 14.7 %scatter_custom_fusion.3 = f32[512]{0:T(512)S(1)} fusion(s32[2048]{0:T(1024)S(1)} %bitcast.55, f32[2048]{0:T(1024)S(1)} %bitcast.44, f32[]{:T(128)} %constant.12.clone.1), kind=kCustom, calls=%fused_computation.104 | custom fusion | flops 2048 | bytes 2052 | tf_op jit(solution)/shard_map/scatter-add | solution.py:32
  96.8 0.0 copy-start.6
  96.8 0.6 copy-done.6
  97.4 0.6 dynamic-slice
  98.7 0.1 fusion.39
  98.8 4.3 all-gather
  103.1 0.1 fusion.13
  103.2 34.1 %all-reduce.8 = (f32[512]{0:T(512)S(1)}, f32[512]{0:T(512)S(1)}) all-reduce(f32[512]{0:T(512)S(1)} %scatter_custom_fusion.2, f32[512]{0:T(512)S(1)} %scatter_custom_fusion.3), channel_id=1, replica_groups=mesh['tile'=16,'loop'=2] {'tile'}, use_global_device_ids=true, to_apply=%region_6.0 | all-reduce | flops 1024 | bytes 8192 | tf_op jit(solution)/shard_map/psum | solution.py:53
  137.3 11.8 %gather_fusion.2 = f32[2048]{0:T(1024)S(1)} fusion(f32[2048]{0:T(1024)S(1)} %get-tuple-element.34, s32[2048]{0:T(1024)S(1)} %bitcast_clamp_fusion), kind=kCustom, calls=%fused_computation.2 | custom fusion | bytes 24576 | tf_op jit(solution)/shard_map/gather | solution.py:93
  149.1 8.6 %gather_fusion = f32[2048]{0:T(1024)S(1)} fusion(f32[1024]{0:T(1024)S(1)} %bitcast.38, s32[2048]{0:T(1024)S(1)} %bitcast_clamp_fusion.2), kind=kCustom, calls=%fused_computation | custom fusion | bytes 24576 | tf_op jit(solution)/shard_map/gather | solution.py:93
  157.7 13.2 %gather_fusion.1 = f32[2048]{0:T(1024)S(1)} fusion(f32[512]{0:T(512)S(1)} %add_divide_fusion.1, s32[2048]{0:T(1024)S(1)} %bitcast_clamp_fusion.1), kind=kCustom, calls=%fused_computation.1 | custom fusion | bytes 24576 | tf_op jit(solution)/shard_map/gather | solution.py:93
  170.9 14.7 %scatter_custom_fusion.7 = f32[512]{0:T(512)S(1)} fusion(s32[2048]{0:T(1024)S(1)} %bitcast.56, f32[2048]{0:T(1024)S(1)} %add_multiply_fusion.1, f32[]{:T(128)} %constant.12.clone.1), kind=kCustom, calls=%fused_computation.102 | custom fusion | flops 2048 | bytes 2052 | tf_op jit(solution)/shard_map/scatter-add | solution.py:32
  185.6 14.9 %scatter_custom_fusion.6 = f32[1024]{0:T(1024)S(1)} fusion(s32[2048]{0:T(1024)S(1)} %bitcast.60, f32[2048]{0:T(1024)S(1)} %add_multiply_fusion.1, f32[]{:T(128)} %constant.12.clone.1), kind=kCustom, calls=%fused_computation.90 | custom fusion | flops 2048 | bytes 4100 | tf_op jit(solution)/shard_map/scatter-add | solution.py:32
  200.4 11.4 %scatter_custom_fusion.8 = f32[2048]{0:T(1024)S(1)} fusion(s32[2048]{0:T(1024)S(1)} %bitcast.52, f32[2048]{0:T(1024)S(1)} %add_multiply_fusion.1, f32[]{:T(128)} %constant.12.clone.1), kind=kCustom, calls=%fused_computation.63 | custom fusion | flops 2048 | bytes 8196 | tf_op jit(solution)/shard_map/scatter-add | solution.py:32
  211.9 29.5 %psum.89 = f32[512]{0:T(512)S(1)} all-reduce(f32[512]{0:T(512)S(1)} %scatter_custom_fusion.7), channel_id=1, replica_groups=mesh['tile'=16,'loop'=2] {'tile'}, use_global_device_ids=true, to_apply=%region_20.21 | all-reduce | flops 512 | bytes 4096 | tf_op jit(solution)/shard_map/psum | solution.py:53
  241.4 7.2 %all-reduce.10 = (f32[1024]{0:T(1024)S(1)}, f32[8,256]{1,0:T(8,128)S(1)}) all-reduce(f32[1024]{0:T(1024)S(1)} %scatter_custom_fusion.6, f32[8,256]{1,0:T(8,128)S(1)} %reshape.193), channel_id=4, replica_groups=mesh['tile'=16,'loop'=2] {'loop'}, use_global_device_ids=true, to_apply=%region_17.0.clone | all-reduce | flops 3072 | bytes 24576
  248.5 0.7 multiply_reduce_fusion.7
  249.2 0.7 multiply_reduce_fusion.6
  253.1 0.0 collective-permute-done.1
  253.1 0.0 collective-permute-done
  253.1 0.7 multiply_reduce_fusion.1
  254.5 36.9 %all-reduce.7 = (f32[]{:T(128)}, f32[]{:T(128)}) all-reduce(f32[]{:T(128)S(6)} %add.286, f32[]{:T(128)S(6)} %add.305), channel_id=1, replica_groups=mesh['tile'=16,'loop'=2] {'tile','loop'}, use_global_device_ids=true, to_apply=%region_15.0 | all-reduce | flops 2 | bytes 16 | tf_op jit(solution)/shard_map/psum | solution.py:125
  292.7 0.1 fusion.38
  292.8 11.8 %gather_fusion.5 = f32[2048]{0:T(1024)S(1)} fusion(f32[2048]{0:T(1024)S(1)} %bitcast.40, s32[2048]{0:T(1024)S(1)} %bitcast_clamp_fusion), kind=kCustom, calls=%fused_computation.5 | custom fusion | bytes 24576 | tf_op jit(solution)/shard_map/gather | solution.py:93
  304.6 4.8 %all-gather.1 = f32[2,1,512]{2,1,0:T(1,128)S(1)} all-gather(f32[1,1,512]{2,1,0:T(1,128)S(1)} %bitcast.47), channel_id=1, replica_groups=mesh['tile'=16,'loop'=2] {'loop'}, dimensions={0}, use_global_device_ids=true | all-gather | bytes 6144 | tf_op jit(solution)/shard_map/all_gather | solution.py:89
  309.4 8.6 %gather_fusion.3 = f32[2048]{0:T(1024)S(1)} fusion(f32[1024]{0:T(1024)S(1)} %bitcast.39, s32[2048]{0:T(1024)S(1)} %bitcast_clamp_fusion.2), kind=kCustom, calls=%fused_computation.3 | custom fusion | bytes 24576 | tf_op jit(solution)/shard_map/gather | solution.py:93
  317.9 13.2 %gather_fusion.4 = f32[2048]{0:T(1024)S(1)} fusion(f32[512]{0:T(512)S(1)} %get-tuple-element.27, s32[2048]{0:T(1024)S(1)} %bitcast_clamp_fusion.1), kind=kCustom, calls=%fused_computation.4 | custom fusion | bytes 24576 | tf_op jit(solution)/shard_map/gather | solution.py:93
  331.2 14.7 %scatter_custom_fusion.9 = f32[1024]{0:T(1024)S(1)} fusion(s32[2048]{0:T(1024)S(1)} %bitcast.61, f32[2048]{0:T(1024)S(1)} %add_multiply_fusion, f32[]{:T(128)} %constant.12.clone.1), kind=kCustom, calls=%fused_computation.88 | custom fusion | flops 2048 | bytes 4100 | tf_op jit(solution)/shard_map/scatter-add | solution.py:32
  345.9 11.4 %scatter_custom_fusion.11 = f32[2048]{0:T(1024)S(1)} fusion(s32[2048]{0:T(1024)S(1)} %bitcast.53, f32[2048]{0:T(1024)S(1)} %add_multiply_fusion, f32[]{:T(128)} %constant.12.clone.1), kind=kCustom, calls=%fused_computation.61 | custom fusion | flops 2048 | bytes 8196 | tf_op jit(solution)/shard_map/scatter-add | solution.py:32
  357.3 14.7 %scatter_custom_fusion.10 = f32[512]{0:T(512)S(1)} fusion(s32[2048]{0:T(1024)S(1)} %bitcast.57, f32[2048]{0:T(1024)S(1)} %add_multiply_fusion, f32[]{:T(128)} %constant.12.clone.1), kind=kCustom, calls=%fused_computation.100 | custom fusion | flops 2048 | bytes 2052 | tf_op jit(solution)/shard_map/scatter-add | solution.py:32
  372.0 30.6 %psum.93 = f32[512]{0:T(512)S(1)} all-reduce(f32[512]{0:T(512)S(1)} %scatter_custom_fusion.10), channel_id=1, replica_groups=mesh['tile'=16,'loop'=2] {'tile'}, use_global_device_ids=true, to_apply=%region_34.35 | all-reduce | flops 512 | bytes 4096 | tf_op jit(solution)/shard_map/psum | solution.py:53
  402.6 1.3 collective-permute-start.3
  403.9 1.3 collective-permute-start.2
  405.2 7.9 %all-reduce.9 = (f32[1024]{0:T(1024)S(1)}, f32[8,256]{1,0:T(8,128)S(1)}) all-reduce(f32[1024]{0:T(1024)S(1)} %scatter_custom_fusion.9, f32[8,256]{1,0:T(8,128)S(1)} %reshape.196), channel_id=5, replica_groups=mesh['tile'=16,'loop'=2] {'loop'}, use_global_device_ids=true, to_apply=%region_31.32.clone | all-reduce | flops 3072 | bytes 24576
  413.1 0.6 multiply_reduce_fusion.3
  413.7 0.8 fusion.29
  417.0 0.0 collective-permute-done.3
  417.0 0.0 collective-permute-done.2
  417.0 0.8 fusion.18
  419.1 37.3 %all-reduce.6 = (f32[]{:T(128)}, f32[]{:T(128)}) all-reduce(f32[]{:T(128)S(6)} %add.310, f32[]{:T(128)S(6)} %add.322), channel_id=1, replica_groups=mesh['tile'=16,'loop'=2] {'tile','loop'}, use_global_device_ids=true, to_apply=%region_29.30 | all-reduce | flops 2 | bytes 16 | tf_op jit(solution)/shard_map/psum | solution.py:125
  461.1 0.6 multiply_add_fusion.2
  461.7 0.6 multiply_add_fusion
  (29 shorter events, 0.2 us)
Async XLA Ops:
  0.6 0.7 copy-start.5
  0.7 0.7 copy-start
  0.7 0.7 copy-start.2
  1.4 0.7 copy-start.1
  2.2 29.4 %copy-start.3 = (s32[1,16,128]{2,1,0:T(8,128)S(1)}, s32[1,16,128]{2,1,0:T(8,128)}, u32[]{:S(2)}) copy-start(s32[1,16,128]{2,1,0:T(8,128)} %param.9) | copy-start | bytes 24580
  64.7 2.6 copy-start.4
  64.7 188.4 %collective-permute-start.1 = (f32[1,256]{1,0:T(1,128)S(1)}, f32[1,256]{1,0:T(1,128)S(1)}, u32[]{:S(2)}, u32[]{:S(2)}) collective-permute-start(f32[1,256]{1,0:T(1,128)S(1)} %get-tuple-element.38), channel_id=1, source_target_pairs={{0,2},{2,4},{4,6},{6,8},{8,10},{10,12},{12,14},{14,16},{16,18},{18... | collective-permute-start | bytes 3080 | tf_op jit(solution)/shard_map/ppermute | solution.py:25
  66.0 187.1 %collective-permute-start = (f32[1,256]{1,0:T(1,128)S(1)}, f32[1,256]{1,0:T(1,128)S(1)}, u32[]{:S(2)}, u32[]{:S(2)}) collective-permute-start(f32[1,256]{1,0:T(1,128)S(1)} %get-tuple-element.37), channel_id=1, source_target_pairs={{2,0},{4,2},{6,4},{8,6},{10,8},{12,10},{14,12},{16,14},{18,16},{20... | collective-permute-start | bytes 3080 | tf_op jit(solution)/shard_map/ppermute | solution.py:26
  96.8 0.7 copy-start.6
  402.6 14.4 %collective-permute-start.3 = (f32[1,256]{1,0:T(1,128)S(1)}, f32[1,256]{1,0:T(1,128)S(1)}, u32[]{:S(2)}, u32[]{:S(2)}) collective-permute-start(f32[1,256]{1,0:T(1,128)S(1)} %get-tuple-element.36), channel_id=1, source_target_pairs={{0,2},{2,4},{4,6},{6,8},{8,10},{10,12},{12,14},{14,16},{16,18},{18... | collective-permute-start | bytes 3080 | tf_op jit(solution)/shard_map/ppermute | solution.py:25
  403.9 13.2 %collective-permute-start.2 = (f32[1,256]{1,0:T(1,128)S(1)}, f32[1,256]{1,0:T(1,128)S(1)}, u32[]{:S(2)}, u32[]{:S(2)}) collective-permute-start(f32[1,256]{1,0:T(1,128)S(1)} %get-tuple-element.35), channel_id=1, source_target_pairs={{2,0},{4,2},{6,4},{8,6},{10,8},{12,10},{14,12},{16,14},{18,16},{20... | collective-permute-start | bytes 3080 | tf_op jit(solution)/shard_map/ppermute | solution.py:26
where the time goes:
time: 464 us; the launch traced here: 462 us
  blocking collectives  202 us (44%)
  other arithmetic  170 us (37%)
  local copies, waits for them, and re-layouts  69.9 us (15%)
  between operations  15.4 us (3%)
  starting transfers between devices  5.15 us (1%)
    scatter-add x12, other arithmetic, scatter_add(): jax.ops.segment_sum(values.reshape(-1), targets.reshape(-1), num_segments...  163 us
    psum x3, blocking collectives, exposure_total(): return lax.psum(parts, 'tile')  94.2 us
    psum x2, blocking collectives, paired(): lax.psum((inner_local(current, precon), inner_local(image, precon)), ('ti...  74.2 us
    gather x2, local copies, waits for them, and re-layouts, operate(): expo_dir[expo_ids]  26.4 us
    unnamed x3, blocking collectives  24.8 us
    gather x2, local copies, waits for them, and re-layouts, operate(): flat_line[pixel_ids]  23.6 us
    gather x2, local copies, waits for them, and re-layouts, operate(): piece[nearby] + expo_dir[expo_ids] + flat_line[pixel_ids]  17.2 us
  transfers between devices with their start and end apart: 4, of which 0 were waited for; matrix products, arithmetic and copies ran while one was open for 23% of the time, Pallas kernels for 0%

commit v1 on v0

v1 whole, which is shorter than its diff:
```python
import functools

import jax
import jax.numpy as jnp
from jax import lax
from jax.experimental import pallas as pl
from jax.experimental.pallas import tpu as pltpu
from jax.sharding import PartitionSpec as P

FC = 256
ROWS_DEV = 8
SBLK_DEV = 2
EXP_DEV = 512
STAR_BLK = 256

SMOOTH = 2.0
RIDGE = 0.5

LANES = 128
HALVES = FC // LANES
STAR_ROWS = SBLK_DEV * STAR_BLK // LANES
EXPO_ROWS = EXP_DEV // LANES
FLAT_ROWS = HALVES * ROWS_DEV
MESH = pl.DeviceIdType.MESH
F32 = jnp.float32
BF16 = jnp.bfloat16


def pieces(values):
    high = values.astype(BF16)
    low = (values - high.astype(F32)).astype(BF16)
    return high, low


def fold(items):
    total = items[0]
    for item in items[1:]:
        total = total + item
    return total


def lane_fold(row):
    row = jnp.sum(row, axis=0, keepdims=True)
    return fold([row[:, at : at + LANES] for at in range(0, row.shape[1], LANES)])


def line(rows):
    return jnp.concatenate([rows[b : b + 1, :] for b in range(rows.shape[0])], axis=1)


def beside_columns(flat):
    column = lax.broadcasted_iota(jnp.int32, flat.shape, 1)
    left = jnp.where(column == 0, 0.0, pltpu.roll(flat, 1, 1))
    right = jnp.where(column == FC - 1, 0.0, pltpu.roll(flat, FC - 1, 1))
    return left + right


def kernel(
    tiles, loops,
    slot_ref, block_ref, expo_ref, pixel_ref, mag_ref, weight_ref,
    star_out, expo_out, flat_out,
    hot, mask, edges0, edges1, ext,
    loop0, loop1, expo0, expo1, halo0, halo1, dots0, dots1,
    send, recv,
):
    tile = lax.axis_index("tile")
    loop = lax.axis_index("loop")
    everyone = tiles * loops
    rank = tile * loops + loop
    blocks = slot_ref.shape[1]
    per_shard = blocks // loops
    star_rows = loops * STAR_ROWS
    expo_at = star_rows
    flat_at = star_rows + 8
    rows = flat_at + FLAT_ROWS

    def other(d):
        peer = lax.rem(rank + d, everyone)
        return peer // loops, lax.rem(peer, loops)

    barrier = pltpu.get_barrier_semaphore()

    def greet(d, carry):
        pl.semaphore_signal(barrier, inc=1, device_id=other(d), device_id_type=MESH)
        return carry

    lax.fori_loop(1, everyone, greet, 0)

    def push(src, dst, which, device):
        pltpu.make_async_remote_copy(
            src_ref=src, dst_ref=dst, send_sem=send.at[which], recv_sem=recv.at[which],
            device_id=device, device_id_type=MESH,
        ).start()

    def settle(buffer, count, sem):
        part = buffer.at[pl.ds(0, count)]
        pltpu.make_async_copy(part, part, sem).wait()

    def push_tiles(buffer, which):
        def step(d, carry):
            push(buffer.at[tile], buffer.at[tile], which, (lax.rem(tile + d, tiles), loop))
            return carry

        lax.fori_loop(1, tiles, step, 0)

    def push_loops(buffer, which):
        for d in range(1, loops):
            push(buffer.at[loop], buffer.at[loop], which, (tile, lax.rem(loop + d, loops)))

    def push_edges(edges, buffer, which):
        above = lax.rem(tile + tiles - 1, tiles)
        below = lax.rem(tile + 1, tiles)
        for d in range(loops):
            to = lax.rem(loop + d, loops)
            push(edges, buffer.at[loops + loop], which, (above, to))
            push(edges, buffer.at[loop], which, (below, to))

    def push_dots(buffer, which):
        def step(d, carry):
            push(buffer.at[rank], buffer.at[rank], which, other(d))
            return carry

        lax.fori_loop(1, everyone, step, 0)

    lane_ids = lax.broadcasted_iota(jnp.int32, (LANES, LANES), 0)
    star_ids = lax.broadcasted_iota(jnp.int32, (star_rows, LANES), 0)
    expo_ids = lax.broadcasted_iota(jnp.int32, (8, LANES), 0)
    flat_ids = lax.broadcasted_iota(jnp.int32, (FLAT_ROWS, LANES), 0)
    for b in range(blocks):
        at = slice(b * LANES, (b + 1) * LANES)
        star = block_ref[0, b] * STAR_BLK + slot_ref[0, b : b + 1, :]
        expo = expo_ref[0, b : b + 1, :]
        pixel = pixel_ref[0, b : b + 1, :]
        for k, ids in enumerate((star, expo, pixel)):
            hot[k * LANES : (k + 1) * LANES, at] = jnp.where(
                lane_ids == (ids & (LANES - 1)), 1.0, 0.0
            ).astype(BF16)
        star_high = (b // per_shard) * STAR_ROWS + star // LANES
        pixel_high = (pixel // LANES) % HALVES * ROWS_DEV + pixel // FC
        mask[0:star_rows, at] = jnp.where(star_ids == star_high, 1.0, 0.0)
        mask[expo_at : expo_at + 8, at] = jnp.where(expo_ids == expo // LANES, 1.0, 0.0)
        mask[flat_at:rows, at] = jnp.where(flat_ids == pixel_high, 1.0, 0.0)

    weights = line(weight_ref[0])
    weighted = weights * line(mag_ref[0])

    def scatter(*values):
        parts = []
        for value in values:
            for piece in pieces(value):
                parts.append((mask[...] * piece.astype(F32)).astype(BF16))
        sums = lax.dot_general(
            jnp.concatenate(parts, axis=0), hot[...], (((1,), (1,)), ((), ())),
            preferred_element_type=F32,
        )
        out = []
        for k in range(len(values)):
            both = sums[2 * k * rows : (2 * k + 1) * rows] + sums[(2 * k + 1) * rows : (2 * k + 2) * rows]
            flat = both[flat_at:rows, 2 * LANES : 3 * LANES]
            flat = jnp.concatenate(
                [flat[h * ROWS_DEV : (h + 1) * ROWS_DEV] for h in range(HALVES)], axis=1
            )
            out.append((
                both[0:star_rows, 0:LANES],
                both[expo_at : expo_at + EXPO_ROWS, LANES : 2 * LANES],
                flat,
            ))
        return out

    def gather(star, expo, flat):
        flat = jnp.concatenate([flat[:, h * LANES : (h + 1) * LANES] for h in range(HALVES)], axis=0)
        expo = jnp.concatenate([expo, jnp.zeros((8 - EXPO_ROWS, LANES), F32)], axis=0)

        def place(part, k):
            return jnp.concatenate(
                [part if j == k else jnp.zeros_like(part) for j in range(3)], axis=1
            )

        values = jnp.concatenate([place(star, 0), place(expo, 1), place(flat, 2)], axis=0)
        found = jnp.dot(
            jnp.concatenate(pieces(values), axis=0), hot[...], preferred_element_type=F32
        )
        return jnp.sum((found[0:rows] + found[rows:]) * mask[...], axis=0, keepdims=True)

    (rhs, count) = scatter(weighted, weights)
    expo0[tile] = jnp.concatenate([rhs[1], count[1]], axis=0)
    loop0[loop] = jnp.concatenate(
        [rhs[0], count[0]]
        + [part[2][:, h * LANES : (h + 1) * LANES] for part in (rhs, count) for h in range(HALVES)],
        axis=0,
    )
    edges0[0:2] = rhs[2][0:2]
    edges0[2:4] = count[2][0:2]
    edges0[4:6] = rhs[2][ROWS_DEV - 2 :]
    edges0[6:8] = count[2][ROWS_DEV - 2 :]
    pl.semaphore_wait(barrier, everyone - 1)
    push_tiles(expo0, 0)
    push_edges(edges0, halo0, 2)
    push_loops(loop0, 1)

    settle(loop0, loops - 1, recv.at[1])
    joint = fold([loop0[l] for l in range(loops)])
    rhs_star = joint[0:star_rows]
    diag_star = joint[star_rows : 2 * star_rows] + RIDGE
    joint = joint[2 * star_rows :]
    rhs_mine, count_mine = [
        jnp.concatenate(
            [joint[(k * HALVES + h) * ROWS_DEV : (k * HALVES + h + 1) * ROWS_DEV] for h in range(HALVES)],
            axis=1,
        )
        for k in range(2)
    ]
    settle(halo0, 2 * loops, recv.at[2])
    over = fold([halo0[l] for l in range(loops)])
    under = fold([halo0[loops + l] for l in range(loops)])
    over = jnp.where(tile > 0, over, 0.0)
    under = jnp.where(tile < tiles - 1, under, 0.0)
    inner = slice(2, 2 + ROWS_DEV)
    wide = slice(1, 3 + ROWS_DEV)
    whole = slice(0, 4 + ROWS_DEV)
    ext[0, inner] = rhs_mine
    ext[0, 0:2] = over[4:6]
    ext[0, 2 + ROWS_DEV : 4 + ROWS_DEV] = under[0:2]
    ext[1, inner] = count_mine
    ext[1, 0:2] = over[6:8]
    ext[1, 2 + ROWS_DEV : 4 + ROWS_DEV] = under[2:4]
    ext[2, whole] = ext[0, whole] / (ext[1, whole] + (4.0 * SMOOTH + RIDGE))
    g_star = rhs_star / diag_star
    g_flat = ext[2, inner]
    settle(expo0, tiles - 1, recv.at[0])
    joint = fold([expo0[t] for t in range(tiles)])
    rhs_expo = joint[0:EXPO_ROWS]
    diag_expo = joint[EXPO_ROWS:] + RIDGE
    g_expo = rhs_expo / diag_expo

    shard_row = lax.broadcasted_iota(jnp.int32, (star_rows, LANES), 0) // STAR_ROWS
    own_star = jnp.where(shard_row == loop, 1.0, 0.0)
    own_expo = jnp.where(tile == 0, 1.0, 0.0)
    own_flat = jnp.where(loop == 0, 1.0, 0.0)

    def inner_rows(star, expo, flat):
        return (
            lane_fold(own_star * star) + own_expo * lane_fold(expo) + own_flat * lane_fold(flat)
        )

    fitted = gather(g_star, g_expo, g_flat)
    pulled = weights * fitted
    ((sum_star, sum_expo, sum_flat),) = scatter(pulled)
    expo1[tile, 0:EXPO_ROWS] = sum_expo
    loop1[loop] = jnp.concatenate(
        [sum_star] + [sum_flat[:, h * LANES : (h + 1) * LANES] for h in range(HALVES)], axis=0
    )
    edges1[0:1] = sum_flat[0:1]
    edges1[1:2] = sum_flat[ROWS_DEV - 1 :]
    push_tiles(expo1, 3)
    push_edges(edges1, halo1, 5)
    push_loops(loop1, 4)
    v = ext[2, wide]
    smooth = SMOOTH * (4.0 * v - ext[2, 0 : 2 + ROWS_DEV] - ext[2, 2 : 4 + ROWS_DEV] - beside_columns(v)) + RIDGE * v
    ext[3, wide] = smooth
    smooth_mine = ext[3, inner]
    dots0[rank, 0:1] = inner_rows(rhs_star * g_star, rhs_expo * g_expo, rhs_mine * g_flat)
    dots0[rank, 1:2] = lane_fold(pulled * fitted) + inner_rows(
        RIDGE * g_star * g_star, RIDGE * g_expo * g_expo, smooth_mine * g_flat
    )
    push_dots(dots0, 6)

    settle(loop1, loops - 1, recv.at[4])
    joint = fold([loop1[l] for l in range(loops)])
    image_star = joint[0:star_rows] + RIDGE * g_star
    sum_mine = jnp.concatenate(
        [joint[star_rows + h * ROWS_DEV : star_rows + (h + 1) * ROWS_DEV] for h in range(HALVES)], axis=1
    )
    settle(halo1, 2 * loops, recv.at[5])
    over = fold([halo1[l] for l in range(loops)])
    under = fold([halo1[loops + l] for l in range(loops)])
    ext[4, inner] = sum_mine
    ext[4, 1:2] = over[1:2]
    ext[4, 2 + ROWS_DEV : 3 + ROWS_DEV] = under[0:1]
    row = lax.broadcasted_iota(jnp.int32, (2 + ROWS_DEV, FC), 0)
    inside = ((row > 0) | (tile > 0)) & ((row < 1 + ROWS_DEV) | (tile < tiles - 1))
    image_wide = jnp.where(inside, ext[4, wide] + smooth, 0.0)
    settle(expo1, tiles - 1, recv.at[3])
    joint = fold([expo1[t, 0:EXPO_ROWS] for t in range(tiles)])
    image_expo = joint + RIDGE * g_expo

    def total(buffer, which, count):
        settle(buffer, everyone - 1, recv.at[which])
        joint = fold([buffer[r] for r in range(everyone)])
        return [jnp.sum(joint[k : k + 1], axis=1, keepdims=True) for k in range(count)]

    norm, curve = total(dots0, 6, 2)
    alpha = norm / curve

    res_star = rhs_star - alpha * image_star
    res_expo = rhs_expo - alpha * image_expo
    res_wide = ext[0, wide] - alpha * image_wide
    h_star = res_star / diag_star
    h_expo = res_expo / diag_expo
    ext[5, wide] = res_wide / (ext[1, wide] + (4.0 * SMOOTH + RIDGE))
    ext[6, wide] = res_wide
    ext[7, wide] = image_wide
    h_flat = ext[5, inner]
    fitted = gather(h_star, h_expo, h_flat)
    beside = ext[5, 1 : 1 + ROWS_DEV] + ext[5, 3 : 3 + ROWS_DEV] + beside_columns(h_flat)
    dots1[rank, 0:1] = inner_rows(res_star * h_star, res_expo * h_expo, ext[6, inner] * h_flat)
    dots1[rank, 1:2] = inner_rows(image_star * h_star, image_expo * h_expo, ext[7, inner] * h_flat)
    dots1[rank, 2:3] = lane_fold(weights * fitted * fitted) + inner_rows(
        RIDGE * h_star * h_star,
        RIDGE * h_expo * h_expo,
        (SMOOTH * (4.0 * h_flat - beside) + RIDGE * h_flat) * h_flat,
    )
    push_dots(dots1, 7)
    norm_next, cross, curve_next = total(dots1, 7, 3)
    ratio = norm_next / norm
    step = norm_next / (curve_next + ratio * (2.0 * cross + ratio * curve))

    def solve(first, second):
        return alpha * first + step * (second + ratio * first)

    star = solve(g_star, h_star)
    star_out[...] = fold([
        jnp.where(loop == l, star[l * STAR_ROWS : (l + 1) * STAR_ROWS], 0.0) for l in range(loops)
    ])
    expo_out[...] = solve(g_expo, h_expo)
    flat_out[...] = solve(g_flat, h_flat)

    for which, (buffer, count) in enumerate((
        (expo0, tiles - 1), (loop0, loops - 1), (halo0, 2 * loops),
        (expo1, tiles - 1), (loop1, loops - 1), (halo1, 2 * loops),
        (dots0, everyone - 1), (dots1, everyone - 1),
    )):
        settle(buffer, count, send.at[which])


def on_device(tiles, loops, star_slot, star_block, exposure, superpixel, magnitude, weight):
    blocks = star_slot.shape[1]
    seen = blocks * LANES
    star_rows = loops * STAR_ROWS
    rows = star_rows + 8 + FLAT_ROWS
    vmem = pl.BlockSpec(memory_space=pltpu.VMEM)
    star, expo, flat = pl.pallas_call(
        functools.partial(kernel, tiles, loops),
        out_shape=(
            jax.ShapeDtypeStruct((STAR_ROWS, LANES), F32),
            jax.ShapeDtypeStruct((EXPO_ROWS, LANES), F32),
            jax.ShapeDtypeStruct((ROWS_DEV, FC), F32),
        ),
        in_specs=[vmem, pl.BlockSpec(memory_space=pltpu.SMEM)] + [vmem] * 4,
        out_specs=(vmem, vmem, vmem),
        scratch_shapes=[
            pltpu.VMEM((3 * LANES, seen), BF16),
            pltpu.VMEM((rows, seen), F32),
            pltpu.VMEM((8, FC), F32),
            pltpu.VMEM((8, FC), F32),
            pltpu.VMEM((8, ROWS_DEV + 8, FC), F32),
            pltpu.VMEM((loops, 2 * (star_rows + FLAT_ROWS), LANES), F32),
            pltpu.VMEM((loops, star_rows + FLAT_ROWS, LANES), F32),
            pltpu.VMEM((tiles, 2 * EXPO_ROWS, LANES), F32),
            pltpu.VMEM((tiles, EXPO_ROWS, LANES), F32),
            pltpu.VMEM((2 * loops, 8, FC), F32),
            pltpu.VMEM((2 * loops, 8, FC), F32),
            pltpu.VMEM((tiles * loops, 4, LANES), F32),
            pltpu.VMEM((tiles * loops, 4, LANES), F32),
            pltpu.SemaphoreType.DMA((8,)),
            pltpu.SemaphoreType.DMA((8,)),
        ],
        compiler_params=pltpu.CompilerParams(
            collective_id=0, has_side_effects=True, vmem_limit_bytes=32 * 1024 * 1024
        ),
    )(star_slot, star_block, exposure, superpixel, magnitude, weight)
    return star.reshape(-1), expo.reshape(-1), flat


def solution(mesh):
    in_specs = (
        P("tile", "loop", None),
        P("tile", "loop"),
        P("tile", "loop", None),
        P("tile", "loop", None),
        P("tile", "loop", None),
        P("tile", "loop", None),
    )
    out_specs = (P(("tile", "loop")), P("loop"), P("tile", None))
    return jax.shard_map(
        functools.partial(on_device, mesh.shape["tile"], mesh.shape["loop"]),
        mesh=mesh, in_specs=in_specs, out_specs=out_specs, check_vma=False,
    )
```

time: 464 us -> 29.6 us (0.06)
  blocking collectives: 202 us -> 0 us
  other arithmetic: 170 us -> 0 us
  local copies, waits for them, and re-layouts: 69.9 us -> 5.89 us
  Pallas kernels: 0 us -> 22.6 us
  between operations: 15.4 us -> 0.65 us
  starting transfers between devices: 5.15 us -> 0 us
    psum x5 -> x0, blocking collectives: 168 us -> none  [the longest x3 94.2 us: exposure_total(): return lax.psum(parts, 'tile')]
    scatter-add x12 -> x0, other arithmetic: 163 us -> none  [scatter_add(): jax.ops.segment_sum(values.reshape(-1), targets.reshape(-1), num_segments...]
    gather x6 -> x0, local copies, waits for them, and re-layouts: 67.1 us -> none  [the longest x2 26.4 us: operate(): expo_dir[expo_ids]]
    unnamed x3 -> x0, blocking collectives: 24.8 us -> none
    pallas_call x0 -> x1, Pallas kernels: none -> 22.6 us  [on_device(): pl.pallas_call(functools.partial(kernel, tiles, loops), out_shape=(jax.Sh...]
    all_gather x2 -> x0, blocking collectives: 9.08 us -> none  [operate(): piece = lax.all_gather(star_dir, 'loop', axis=0, tiled=True)]
    ppermute x4 -> x0, starting transfers between devices: 5.15 us -> none  [the longest x2 2.58 us: extended(): after = lax.ppermute(leading, axis, down)]
    reduce_sum x7 -> x0, other arithmetic: 4.8 us -> none  [the longest x3 2.05 us: inner_local(): jnp.sum(first_vec[2] * second_vec[2])]
  transfers between devices with their start and end apart: 4 -> 0, of which waited for: 0 -> 0; matrix products, arithmetic and copies ran while one was open for 23% -> 0% of each run, Pallas kernels for 0% -> 0%
where the time goes in v1:
time: 29.6 us; the launch traced here: 29.1 us
  Pallas kernels  22.6 us (76%)
  local copies, waits for them, and re-layouts  5.89 us (20%)
  between operations  0.65 us (2%)
    pallas_call x1, Pallas kernels, on_device(): pl.pallas_call(functools.partial(kernel, tiles, loops), out_shape=(jax.Sh...  22.6 us
    unnamed x15, local copies, waits for them, and re-layouts  5.89 us

profile of v1, /device:TPU:0, one launch (start us, length us, event | category | flops | bytes accessed | tf_op | source)
XLA Modules:
  0.0 29.1 jit_solution(6266741160917076805)
XLA Ops:
  0.6 0.0 copy-start
  0.6 0.7 %copy-done = s32[1,16,128]{2,1,0:T(8,128)S(1)} copy-done((s32[1,16,128]{2,1,0:T(8,128)S(1)}, s32[1,16,128]{2,1,0:T(8,128)}, u32[]{:S(2)}) %copy-start) | copy-done | bytes 8216
  1.3 0.0 copy-start.1
  1.3 0.7 %copy-done.1 = s32[1,16,128]{2,1,0:T(8,128)S(1)} copy-done((s32[1,16,128]{2,1,0:T(8,128)S(1)}, s32[1,16,128]{2,1,0:T(8,128)}, u32[]{:S(2)}) %copy-start.1) | copy-done | bytes 8216
  2.0 0.0 copy-start.2
  2.0 0.7 %copy-done.2 = s32[1,16,128]{2,1,0:T(8,128)S(1)} copy-done((s32[1,16,128]{2,1,0:T(8,128)S(1)}, s32[1,16,128]{2,1,0:T(8,128)}, u32[]{:S(2)}) %copy-start.2) | copy-done | bytes 8216
  2.7 0.0 copy-start.3
  2.7 0.7 %copy-done.3 = f32[1,16,128]{2,1,0:T(8,128)S(1)} copy-done((f32[1,16,128]{2,1,0:T(8,128)S(1)}, f32[1,16,128]{2,1,0:T(8,128)}, u32[]{:S(2)}) %copy-start.3) | copy-done | bytes 8216
  3.4 0.0 copy-start.4
  3.4 0.7 %copy-done.4 = f32[1,16,128]{2,1,0:T(8,128)S(1)} copy-done((f32[1,16,128]{2,1,0:T(8,128)S(1)}, f32[1,16,128]{2,1,0:T(8,128)}, u32[]{:S(2)}) %copy-start.4) | copy-done | bytes 8216
  4.1 0.0 copy-start.5
  4.1 0.7 %copy-done.5 = s32[1,16]{1,0:T(1,128)S(1)} copy-done((s32[1,16]{1,0:T(1,128)S(1)}, s32[1,16]{1,0:T(1,128)}, u32[]{:S(2)}) %copy-start.5) | copy-done | bytes 88
  4.8 22.6 %shard_map.85 = (f32[4,128]{1,0:T(4,128)S(1)}, f32[4,128]{1,0:T(4,128)S(1)}, f32[8,256]{1,0:T(8,128)S(1)}) custom-call(s32[1,16,128]{2,1,0:T(8,128)S(1)} %copy-done, s32[1,16]{1,0:T(1,128)S(1)} %copy-done.5, s32[1,16,128]{2,1,0:T(8,128)S(1)} %copy-done.1, s32[1,16,128]{2,1,0:T(8,128)S(1)} %copy-done.2, f32[1,16,128]{2,1,0:T(8,128)S(1)} %copy-done.3, ...), custom_call_target="tpu_custom_call" | custom-call | tf_op jit(solution)/shard_map/pallas_call | solution.py:342
  27.4 0.6 %copy.12 = f32[512]{0:T(512)} copy(f32[512]{0:T(512)S(1)} %bitcast.3) | data formatting | bytes 4096
  28.0 0.6 %copy.13 = f32[512]{0:T(512)} copy(f32[512]{0:T(512)S(1)} %bitcast.2) | data formatting | bytes 4096
  28.5 0.6 %copy.14 = f32[8,256]{1,0:T(8,128)} copy(f32[8,256]{1,0:T(8,128)S(1)} %get-tuple-element.14) | data formatting | bytes 16384
Async XLA Ops:
  0.6 0.7 %copy-start = (s32[1,16,128]{2,1,0:T(8,128)S(1)}, s32[1,16,128]{2,1,0:T(8,128)}, u32[]{:S(2)}) copy-start(s32[1,16,128]{2,1,0:T(8,128)} %slot_ref.1) | copy-start | bytes 24580
  1.3 0.7 %copy-start.1 = (s32[1,16,128]{2,1,0:T(8,128)S(1)}, s32[1,16,128]{2,1,0:T(8,128)}, u32[]{:S(2)}) copy-start(s32[1,16,128]{2,1,0:T(8,128)} %expo_ref.1) | copy-start | bytes 24580
  2.0 0.7 %copy-start.2 = (s32[1,16,128]{2,1,0:T(8,128)S(1)}, s32[1,16,128]{2,1,0:T(8,128)}, u32[]{:S(2)}) copy-start(s32[1,16,128]{2,1,0:T(8,128)} %pixel_ref.1) | copy-start | bytes 24580
  2.7 0.7 %copy-start.3 = (f32[1,16,128]{2,1,0:T(8,128)S(1)}, f32[1,16,128]{2,1,0:T(8,128)}, u32[]{:S(2)}) copy-start(f32[1,16,128]{2,1,0:T(8,128)} %mag_ref.1) | copy-start | bytes 24580
  3.4 0.7 %copy-start.4 = (f32[1,16,128]{2,1,0:T(8,128)S(1)}, f32[1,16,128]{2,1,0:T(8,128)}, u32[]{:S(2)}) copy-start(f32[1,16,128]{2,1,0:T(8,128)} %weight_ref.1) | copy-start | bytes 24580
  4.1 0.7 %copy-start.5 = (s32[1,16]{1,0:T(1,128)S(1)}, s32[1,16]{1,0:T(1,128)}, u32[]{:S(2)}) copy-start(s32[1,16]{1,0:T(1,128)} %block_ref.1) | copy-start | bytes 196

commit v2 on v1

--- a/solution.py
+++ b/solution.py
@@ -17,6 +17,7 @@
 RIDGE = 0.5
 
 LANES = 128
+HALF = LANES // 2
 HALVES = FC // LANES
 STAR_ROWS = SBLK_DEV * STAR_BLK // LANES
 EXPO_ROWS = EXP_DEV // LANES
@@ -27,9 +28,8 @@
 
 
 def pieces(values):
-    high = values.astype(BF16)
-    low = (values - high.astype(F32)).astype(BF16)
-    return high, low
+    high = values.astype(BF16).astype(F32)
+    return high, values - high
 
 
 def fold(items):
@@ -57,8 +57,9 @@
 
 def kernel(
     tiles, loops,
-    slot_ref, block_ref, expo_ref, pixel_ref, mag_ref, weight_ref,
+    slot_in, block_in, expo_in, pixel_in, mag_in, weight_in,
     star_out, expo_out, flat_out,
+    slot_ref, block_ref, expo_ref, pixel_ref, mag_ref, weight_ref, load,
     hot, mask, edges0, edges1, ext,
     loop0, loop1, expo0, expo1, halo0, halo1, dots0, dots1,
     send, recv,
@@ -69,22 +70,40 @@
     rank = tile * loops + loop
     blocks = slot_ref.shape[1]
     per_shard = blocks // loops
-    star_rows = loops * STAR_ROWS
+    star_wide = loops * STAR_ROWS
+    star_rows = 2 * star_wide
     expo_at = star_rows
-    flat_at = star_rows + 8
+    flat_at = star_rows + 2 * EXPO_ROWS
     rows = flat_at + FLAT_ROWS
 
-    def other(d):
-        peer = lax.rem(rank + d, everyone)
-        return peer // loops, lax.rem(peer, loops)
+    loads = [
+        pltpu.make_async_copy(src, dst, load.at[k])
+        for k, (src, dst) in enumerate((
+            (slot_in, slot_ref), (block_in, block_ref), (expo_in, expo_ref),
+            (pixel_in, pixel_ref), (weight_in, weight_ref), (mag_in, mag_ref),
+        ))
+    ]
+    for copy in loads:
+        copy.start()
+
+    def turn(index, d, size):
+        index = index + d
+        return jnp.where(index >= size, index - size, index)
+
+    def each_other(act):
+        for k in range(loops):
+            to = turn(loop, k, loops)
+
+            def step(d, carry, to=to):
+                act((turn(tile, d, tiles), to))
+                return carry
+
+            lax.fori_loop(0 if k else 1, tiles, step, 0)
 
     barrier = pltpu.get_barrier_semaphore()
-
-    def greet(d, carry):
-        pl.semaphore_signal(barrier, inc=1, device_id=other(d), device_id_type=MESH)
-        return carry
-
-    lax.fori_loop(1, everyone, greet, 0)
+    each_other(
+        lambda device: pl.semaphore_signal(barrier, inc=1, device_id=device, device_id_type=MESH)
+    )
 
     def push(src, dst, which, device):
         pltpu.make_async_remote_copy(
@@ -98,87 +117,102 @@
 
     def push_tiles(buffer, which):
         def step(d, carry):
-            push(buffer.at[tile], buffer.at[tile], which, (lax.rem(tile + d, tiles), loop))
+            push(buffer.at[tile], buffer.at[tile], which, (turn(tile, d, tiles), loop))
             return carry
 
         lax.fori_loop(1, tiles, step, 0)
 
     def push_loops(buffer, which):
         for d in range(1, loops):
-            push(buffer.at[loop], buffer.at[loop], which, (tile, lax.rem(loop + d, loops)))
+            push(buffer.at[loop], buffer.at[loop], which, (tile, turn(loop, d, loops)))
 
     def push_edges(edges, buffer, which):
-        above = lax.rem(tile + tiles - 1, tiles)
-        below = lax.rem(tile + 1, tiles)
+        above = turn(tile, tiles - 1, tiles)
+        below = turn(tile, 1, tiles)
         for d in range(loops):
-            to = lax.rem(loop + d, loops)
+            to = turn(loop, d, loops)
             push(edges, buffer.at[loops + loop], which, (above, to))
             push(edges, buffer.at[loop], which, (below, to))
 
     def push_dots(buffer, which):
-        def step(d, carry):
-            push(buffer.at[rank], buffer.at[rank], which, other(d))
-            return carry
-
-        lax.fori_loop(1, everyone, step, 0)
-
+        each_other(lambda device: push(buffer.at[rank], buffer.at[rank], which, device))
+
+    half_ids = lax.broadcasted_iota(jnp.int32, (HALF, LANES), 0)
     lane_ids = lax.broadcasted_iota(jnp.int32, (LANES, LANES), 0)
     star_ids = lax.broadcasted_iota(jnp.int32, (star_rows, LANES), 0)
-    expo_ids = lax.broadcasted_iota(jnp.int32, (8, LANES), 0)
+    expo_ids = lax.broadcasted_iota(jnp.int32, (2 * EXPO_ROWS, LANES), 0)
     flat_ids = lax.broadcasted_iota(jnp.int32, (FLAT_ROWS, LANES), 0)
+    for copy in loads:
+        copy.wait()
     for b in range(blocks):
         at = slice(b * LANES, (b + 1) * LANES)
         star = block_ref[0, b] * STAR_BLK + slot_ref[0, b : b + 1, :]
         expo = expo_ref[0, b : b + 1, :]
         pixel = pixel_ref[0, b : b + 1, :]
-        for k, ids in enumerate((star, expo, pixel)):
-            hot[k * LANES : (k + 1) * LANES, at] = jnp.where(
-                lane_ids == (ids & (LANES - 1)), 1.0, 0.0
-            ).astype(BF16)
-        star_high = (b // per_shard) * STAR_ROWS + star // LANES
+        hot[0:HALF, at] = jnp.where(half_ids == (star & (HALF - 1)), 1.0, 0.0).astype(BF16)
+        hot[HALF:LANES, at] = jnp.where(half_ids == (expo & (HALF - 1)), 1.0, 0.0).astype(BF16)
+        hot[LANES : 2 * LANES, at] = jnp.where(lane_ids == (pixel & (LANES - 1)), 1.0, 0.0).astype(BF16)
+        star_high = (
+            (b // per_shard) * (2 * STAR_ROWS) + ((star // HALF) & 1) * STAR_ROWS + star // LANES
+        )
+        expo_high = ((expo // HALF) & 1) * EXPO_ROWS + expo // LANES
         pixel_high = (pixel // LANES) % HALVES * ROWS_DEV + pixel // FC
         mask[0:star_rows, at] = jnp.where(star_ids == star_high, 1.0, 0.0)
-        mask[expo_at : expo_at + 8, at] = jnp.where(expo_ids == expo // LANES, 1.0, 0.0)
+        mask[expo_at:flat_at, at] = jnp.where(expo_ids == expo_high, 1.0, 0.0)
         mask[flat_at:rows, at] = jnp.where(flat_ids == pixel_high, 1.0, 0.0)
 
     weights = line(weight_ref[0])
     weighted = weights * line(mag_ref[0])
 
+    def lower(count):
+        return lax.broadcasted_iota(jnp.int32, (count, LANES), 1) < HALF
+
+    def swap(part):
+        return pltpu.roll(part, HALF, 1)
+
     def scatter(*values):
-        parts = []
-        for value in values:
-            for piece in pieces(value):
-                parts.append((mask[...] * piece.astype(F32)).astype(BF16))
+        parts = jnp.concatenate(
+            [mask[...] * piece for value in values for piece in pieces(value)], axis=0
+        )
         sums = lax.dot_general(
-            jnp.concatenate(parts, axis=0), hot[...], (((1,), (1,)), ((), ())),
-            preferred_element_type=F32,
+            parts.astype(BF16), hot[...], (((1,), (1,)), ((), ())), preferred_element_type=F32
         )
         out = []
         for k in range(len(values)):
             both = sums[2 * k * rows : (2 * k + 1) * rows] + sums[(2 * k + 1) * rows : (2 * k + 2) * rows]
-            flat = both[flat_at:rows, 2 * LANES : 3 * LANES]
-            flat = jnp.concatenate(
-                [flat[h * ROWS_DEV : (h + 1) * ROWS_DEV] for h in range(HALVES)], axis=1
-            )
+            left, flat = both[:, 0:LANES], both[flat_at:rows, LANES:]
+            star = []
+            for at in range(0, star_rows, 2 * STAR_ROWS):
+                low = left[at : at + STAR_ROWS]
+                high = left[at + STAR_ROWS : at + 2 * STAR_ROWS]
+                star.append(jnp.where(lower(STAR_ROWS), low, swap(high)))
+            low, high = left[expo_at : expo_at + EXPO_ROWS], left[expo_at + EXPO_ROWS : flat_at]
             out.append((
-                both[0:star_rows, 0:LANES],
-                both[expo_at : expo_at + EXPO_ROWS, LANES : 2 * LANES],
-                flat,
+                jnp.concatenate(star, axis=0),
+                jnp.where(lower(EXPO_ROWS), swap(low), high),
+                jnp.concatenate(
+                    [flat[h * ROWS_DEV : (h + 1) * ROWS_DEV] for h in range(HALVES)], axis=1
+                ),
             ))
         return out
 
     def gather(star, expo, flat):
-        flat = jnp.concatenate([flat[:, h * LANES : (h + 1) * LANES] for h in range(HALVES)], axis=0)
-        expo = jnp.concatenate([expo, jnp.zeros((8 - EXPO_ROWS, LANES), F32)], axis=0)
-
-        def place(part, k):
-            return jnp.concatenate(
-                [part if j == k else jnp.zeros_like(part) for j in range(3)], axis=1
-            )
-
-        values = jnp.concatenate([place(star, 0), place(expo, 1), place(flat, 2)], axis=0)
+        parts = []
+        for at in range(0, star_wide, STAR_ROWS):
+            part = star[at : at + STAR_ROWS]
+            parts += [part, swap(part)]
+        star = jnp.where(lower(star_rows), jnp.concatenate(parts, axis=0), 0.0)
+        expo = jnp.where(lower(2 * EXPO_ROWS), 0.0, jnp.concatenate([swap(expo), expo], axis=0))
+        left = jnp.concatenate([star, expo, jnp.zeros((FLAT_ROWS, LANES), F32)], axis=0)
+        right = jnp.concatenate(
+            [jnp.zeros((flat_at, LANES), F32)]
+            + [flat[:, h * LANES : (h + 1) * LANES] for h in range(HALVES)],
+            axis=0,
+        )
+        values = jnp.concatenate([left, right], axis=1)
         found = jnp.dot(
-            jnp.concatenate(pieces(values), axis=0), hot[...], preferred_element_type=F32
+            jnp.concatenate(pieces(values), axis=0).astype(BF16), hot[...],
+            preferred_element_type=F32,
         )
         return jnp.sum((found[0:rows] + found[rows:]) * mask[...], axis=0, keepdims=True)
 
@@ -200,9 +234,9 @@
 
     settle(loop0, loops - 1, recv.at[1])
     joint = fold([loop0[l] for l in range(loops)])
-    rhs_star = joint[0:star_rows]
-    diag_star = joint[star_rows : 2 * star_rows] + RIDGE
-    joint = joint[2 * star_rows :]
+    rhs_star = joint[0:star_wide]
+    diag_star = joint[star_wide : 2 * star_wide] + RIDGE
+    joint = joint[2 * star_wide :]
     rhs_mine, count_mine = [
         jnp.concatenate(
             [joint[(k * HALVES + h) * ROWS_DEV : (k * HALVES + h + 1) * ROWS_DEV] for h in range(HALVES)],
@@ -233,7 +267,7 @@
     diag_expo = joint[EXPO_ROWS:] + RIDGE
     g_expo = rhs_expo / diag_expo
 
-    shard_row = lax.broadcasted_iota(jnp.int32, (star_rows, LANES), 0) // STAR_ROWS
+    shard_row = lax.broadcasted_iota(jnp.int32, (star_wide, LANES), 0) // STAR_ROWS
     own_star = jnp.where(shard_row == loop, 1.0, 0.0)
     own_expo = jnp.where(tile == 0, 1.0, 0.0)
     own_flat = jnp.where(loop == 0, 1.0, 0.0)
@@ -267,9 +301,9 @@
 
     settle(loop1, loops - 1, recv.at[4])
     joint = fold([loop1[l] for l in range(loops)])
-    image_star = joint[0:star_rows] + RIDGE * g_star
+    image_star = joint[0:star_wide] + RIDGE * g_star
     sum_mine = jnp.concatenate(
-        [joint[star_rows + h * ROWS_DEV : star_rows + (h + 1) * ROWS_DEV] for h in range(HALVES)], axis=1
+        [joint[star_wide + h * ROWS_DEV : star_wide + (h + 1) * ROWS_DEV] for h in range(HALVES)], axis=1
     )
     settle(halo1, 2 * loops, recv.at[5])
     over = fold([halo1[l] for l in range(loops)])
@@ -289,6 +323,12 @@
         joint = fold([buffer[r] for r in range(everyone)])
         return [jnp.sum(joint[k : k + 1], axis=1, keepdims=True) for k in range(count)]
 
+    ext[7, wide] = image_wide
+    fitted_image = gather(
+        image_star / diag_star,
+        image_expo / diag_expo,
+        ext[7, inner] / (count_mine + (4.0 * SMOOTH + RIDGE)),
+    )
     norm, curve = total(dots0, 6, 2)
     alpha = norm / curve
 
@@ -299,9 +339,8 @@
     h_expo = res_expo / diag_expo
     ext[5, wide] = res_wide / (ext[1, wide] + (4.0 * SMOOTH + RIDGE))
     ext[6, wide] = res_wide
-    ext[7, wide] = image_wide
     h_flat = ext[5, inner]
-    fitted = gather(h_star, h_expo, h_flat)
+    fitted = fitted - alpha * fitted_image
     beside = ext[5, 1 : 1 + ROWS_DEV] + ext[5, 3 : 3 + ROWS_DEV] + beside_columns(h_flat)
     dots1[rank, 0:1] = inner_rows(res_star * h_star, res_expo * h_expo, ext[6, inner] * h_flat)
     dots1[rank, 1:2] = inner_rows(image_star * h_star, image_expo * h_expo, ext[7, inner] * h_flat)
@@ -333,29 +372,49 @@
         settle(buffer, count, send.at[which])
 
 
+def write_kernel(star, expo, flat, star_out, expo_out, flat_out, sems):
+    copies = [
+        pltpu.make_async_copy(src, dst, sems.at[k])
+        for k, (src, dst) in enumerate(((star, star_out), (expo, expo_out), (flat, flat_out)))
+    ]
+    for copy in copies:
+        copy.start()
+    for copy in copies:
+        copy.wait()
+
+
 def on_device(tiles, loops, star_slot, star_block, exposure, superpixel, magnitude, weight):
     blocks = star_slot.shape[1]
     seen = blocks * LANES
-    star_rows = loops * STAR_ROWS
-    rows = star_rows + 8 + FLAT_ROWS
+    star_wide = loops * STAR_ROWS
+    rows = 2 * star_wide + 2 * EXPO_ROWS + FLAT_ROWS
     vmem = pl.BlockSpec(memory_space=pltpu.VMEM)
-    star, expo, flat = pl.pallas_call(
+    hbm = pl.BlockSpec(memory_space=pltpu.HBM)
+    out_shape = (
+        jax.ShapeDtypeStruct((STAR_ROWS, LANES), F32),
+        jax.ShapeDtypeStruct((EXPO_ROWS, LANES), F32),
+        jax.ShapeDtypeStruct((ROWS_DEV, FC), F32),
+    )
+    parts = pl.pallas_call(
         functools.partial(kernel, tiles, loops),
-        out_shape=(
-            jax.ShapeDtypeStruct((STAR_ROWS, LANES), F32),
-            jax.ShapeDtypeStruct((EXPO_ROWS, LANES), F32),
-            jax.ShapeDtypeStruct((ROWS_DEV, FC), F32),
-        ),
-        in_specs=[vmem, pl.BlockSpec(memory_space=pltpu.SMEM)] + [vmem] * 4,
+        out_shape=out_shape,
+        in_specs=[hbm] * 6,
         out_specs=(vmem, vmem, vmem),
         scratch_shapes=[
-            pltpu.VMEM((3 * LANES, seen), BF16),
+            pltpu.VMEM(star_slot.shape, jnp.int32),
+            pltpu.SMEM(star_block.shape, jnp.int32),
+            pltpu.VMEM(exposure.shape, jnp.int32),
+            pltpu.VMEM(superpixel.shape, jnp.int32),
+            pltpu.VMEM(magnitude.shape, F32),
+            pltpu.VMEM(weight.shape, F32),
+            pltpu.SemaphoreType.DMA((6,)),
+            pltpu.VMEM((2 * LANES, seen), BF16),
             pltpu.VMEM((rows, seen), F32),
             pltpu.VMEM((8, FC), F32),
             pltpu.VMEM((8, FC), F32),
             pltpu.VMEM((8, ROWS_DEV + 8, FC), F32),
-            pltpu.VMEM((loops, 2 * (star_rows + FLAT_ROWS), LANES), F32),
-            pltpu.VMEM((loops, star_rows + FLAT_ROWS, LANES), F32),
+            pltpu.VMEM((loops, 2 * (star_wide + FLAT_ROWS), LANES), F32),
+            pltpu.VMEM((loops, star_wide + FLAT_ROWS, LANES), F32),
             pltpu.VMEM((tiles, 2 * EXPO_ROWS, LANES), F32),
             pltpu.VMEM((tiles, EXPO_ROWS, LANES), F32),
             pltpu.VMEM((2 * loops, 8, FC), F32),
@@ -368,7 +427,17 @@
         compiler_params=pltpu.CompilerParams(
             collective_id=0, has_side_effects=True, vmem_limit_bytes=32 * 1024 * 1024
         ),
-    )(star_slot, star_block, exposure, superpixel, magnitude, weight)
+    )(*[
+        pltpu.with_memory_space_constraint(x, pltpu.HBM)
+        for x in (star_slot, star_block, exposure, superpixel, magnitude, weight)
+    ])
+    star, expo, flat = pl.pallas_call(
+        write_kernel,
+        out_shape=out_shape,
+        in_specs=[vmem] * 3,
+        out_specs=(hbm,) * 3,
+        scratch_shapes=[pltpu.SemaphoreType.DMA((3,))],
+    )(*parts)
     return star.reshape(-1), expo.reshape(-1), flat
 
 

time: 29.6 us -> 26.3 us (0.89)
  local copies, waits for them, and re-layouts: 5.89 us -> 1.78 us
  Pallas kernels: 22.6 us -> 23.6 us
    unnamed x15 -> x6, local copies, waits for them, and re-layouts: 5.89 us -> 1.78 us
    pallas_call x1 -> x2, Pallas kernels: 22.6 us -> 23.6 us  [the longest x1 22.2 us: on_device(): pl.pallas_call(functools.partial(kernel, tiles, loops), out_shape=out_sha...]
where the time goes in v2:
time: 26.3 us; the launch traced here: 26 us
  Pallas kernels  23.6 us (90%)
  local copies, waits for them, and re-layouts  1.78 us (7%)
  between operations  0.65 us (2%)
    pallas_call x1, Pallas kernels, on_device(): pl.pallas_call(functools.partial(kernel, tiles, loops), out_shape=out_sha...  22.2 us
    unnamed x6, local copies, waits for them, and re-layouts  1.78 us
    pallas_call x1, Pallas kernels, on_device(): pl.pallas_call(write_kernel, out_shape=out_shape, in_specs=[vmem] * 3, ou...  1.34 us

profile of v2, /device:TPU:0, one launch (start us, length us, event | category | flops | bytes accessed | tf_op | source)
XLA Modules:
  0.0 26.0 jit_solution(2709074258941173343)
XLA Ops:
  0.6 22.2 %shard_map.85 = (f32[4,128]{1,0:T(4,128)S(1)}, f32[4,128]{1,0:T(4,128)S(1)}, f32[8,256]{1,0:T(8,128)S(1)}) custom-call(s32[1,16,128]{2,1,0:T(8,128)} %slot_in.1, s32[1,16]{1,0:T(1,128)} %block_in.1, s32[1,16,128]{2,1,0:T(8,128)} %expo_in.1, s32[1,16,128]{2,1,0:T(8,128)} %pixel_in.1, f32[1,16,128]{2,1,0:T(8,128)} %mag_in.1, f32[1,16,128]{2,1,0:T(8,128)} %weight_in.1), custom_call_target="tpu_custom_call" | custom-call | tf_op jit(solution)/shard_map/pallas_call | solution.py:398
  22.9 0.0 copy-start
  22.9 0.6 %copy-done = f32[8,256]{1,0:T(8,128)} copy-done((f32[8,256]{1,0:T(8,128)}, f32[8,256]{1,0:T(8,128)S(1)}, u32[]{:S(2)}) %copy-start) | copy-done | bytes 8216
  23.5 0.0 copy-start.1
  23.5 0.6 %copy-done.1 = f32[4,128]{1,0:T(4,128)} copy-done((f32[4,128]{1,0:T(4,128)}, f32[4,128]{1,0:T(4,128)S(1)}, u32[]{:S(2)}) %copy-start.1) | copy-done | bytes 2072
  24.1 0.0 copy-start.2
  24.1 0.6 %copy-done.2 = f32[4,128]{1,0:T(4,128)} copy-done((f32[4,128]{1,0:T(4,128)}, f32[4,128]{1,0:T(4,128)S(1)}, u32[]{:S(2)}) %copy-start.2) | copy-done | bytes 2072
  24.7 1.3 %shard_map.86 = (f32[4,128]{1,0:T(4,128)}, f32[4,128]{1,0:T(4,128)}, f32[8,256]{1,0:T(8,128)}) custom-call(f32[4,128]{1,0:T(4,128)} %copy-done.1, f32[4,128]{1,0:T(4,128)} %copy-done.2, f32[8,256]{1,0:T(8,128)} %copy-done), custom_call_target="tpu_custom_call" | custom-call | tf_op jit(solution)/shard_map/pallas_call | solution.py:434
Async XLA Ops:
  22.9 0.6 %copy-start = (f32[8,256]{1,0:T(8,128)}, f32[8,256]{1,0:T(8,128)S(1)}, u32[]{:S(2)}) copy-start(f32[8,256]{1,0:T(8,128)S(1)} %get-tuple-element.11.flat) | copy-start | bytes 24580
  23.5 0.6 %copy-start.1 = (f32[4,128]{1,0:T(4,128)}, f32[4,128]{1,0:T(4,128)S(1)}, u32[]{:S(2)}) copy-start(f32[4,128]{1,0:T(4,128)S(1)} %get-tuple-element.9.star) | copy-start | bytes 6148
  24.1 0.6 %copy-start.2 = (f32[4,128]{1,0:T(4,128)}, f32[4,128]{1,0:T(4,128)S(1)}, u32[]{:S(2)}) copy-start(f32[4,128]{1,0:T(4,128)S(1)} %get-tuple-element.10.expo) | copy-start | bytes 6148

commit v3 on v2

--- a/solution.py
+++ b/solution.py
@@ -61,7 +61,7 @@
     star_out, expo_out, flat_out,
     slot_ref, block_ref, expo_ref, pixel_ref, mag_ref, weight_ref, load,
     hot, mask, edges0, edges1, ext,
-    loop0, loop1, expo0, expo1, halo0, halo1, dots0, dots1,
+    loop0, loop1, wide0, wide1, expo0, expo1, halo0, halo1, dots0, dots1,
     send, recv,
 ):
     tile = lax.axis_index("tile")
@@ -90,15 +90,23 @@
         index = index + d
         return jnp.where(index >= size, index - size, index)
 
+    def span(first, last, act):
+        if last <= 16:
+            for d in range(first, last):
+                act(d)
+            return
+
+        def step(d, carry):
+            act(d)
+            return carry
+
+        lax.fori_loop(first, last, step, 0)
+
     def each_other(act):
         for k in range(loops):
             to = turn(loop, k, loops)
 
-            def step(d, carry, to=to):
-                act((turn(tile, d, tiles), to))
-                return carry
-
-            lax.fori_loop(0 if k else 1, tiles, step, 0)
+            span(0 if k else 1, tiles, lambda d, to=to: act((turn(tile, d, tiles), to)))
 
     barrier = pltpu.get_barrier_semaphore()
     each_other(
@@ -116,11 +124,9 @@
         pltpu.make_async_copy(part, part, sem).wait()
 
     def push_tiles(buffer, which):
-        def step(d, carry):
-            push(buffer.at[tile], buffer.at[tile], which, (turn(tile, d, tiles), loop))
-            return carry
-
-        lax.fori_loop(1, tiles, step, 0)
+        span(1, tiles, lambda d: push(
+            buffer.at[tile], buffer.at[tile], which, (turn(tile, d, tiles), loop)
+        ))
 
     def push_loops(buffer, which):
         for d in range(1, loops):
@@ -170,17 +176,27 @@
     def swap(part):
         return pltpu.roll(part, HALF, 1)
 
-    def scatter(*values):
+    def spread(values, mine, columns):
         parts = jnp.concatenate(
-            [mask[...] * piece for value in values for piece in pieces(value)], axis=0
+            [mask[mine] * piece for value in values for piece in pieces(value)], axis=0
         )
         sums = lax.dot_general(
-            parts.astype(BF16), hot[...], (((1,), (1,)), ((), ())), preferred_element_type=F32
-        )
+            parts.astype(BF16), hot[columns], (((1,), (1,)), ((), ())), preferred_element_type=F32
+        )
+        size = mine.stop - mine.start
+        return [
+            sums[2 * k * size : (2 * k + 1) * size] + sums[(2 * k + 1) * size : (2 * k + 2) * size]
+            for k in range(len(values))
+        ]
+
+    near = slice(0, flat_at)
+    far = slice(flat_at, rows)
+    near_columns = slice(0, LANES)
+    far_columns = slice(LANES, 2 * LANES)
+
+    def scatter_near(*values):
         out = []
-        for k in range(len(values)):
-            both = sums[2 * k * rows : (2 * k + 1) * rows] + sums[(2 * k + 1) * rows : (2 * k + 2) * rows]
-            left, flat = both[:, 0:LANES], both[flat_at:rows, LANES:]
+        for left in spread(values, near, near_columns):
             star = []
             for at in range(0, star_rows, 2 * STAR_ROWS):
                 low = left[at : at + STAR_ROWS]
@@ -188,62 +204,74 @@
                 star.append(jnp.where(lower(STAR_ROWS), low, swap(high)))
             low, high = left[expo_at : expo_at + EXPO_ROWS], left[expo_at + EXPO_ROWS : flat_at]
             out.append((
-                jnp.concatenate(star, axis=0),
-                jnp.where(lower(EXPO_ROWS), swap(low), high),
-                jnp.concatenate(
-                    [flat[h * ROWS_DEV : (h + 1) * ROWS_DEV] for h in range(HALVES)], axis=1
-                ),
+                jnp.concatenate(star, axis=0), jnp.where(lower(EXPO_ROWS), swap(low), high)
             ))
         return out
 
-    def gather(star, expo, flat):
+    def scatter_flat(*values):
+        return spread(values, far, far_columns)
+
+    def in_lines(flat):
+        return jnp.concatenate(
+            [flat[h * ROWS_DEV : (h + 1) * ROWS_DEV] for h in range(HALVES)], axis=1
+        )
+
+    def find(values, mine, columns):
+        size = mine.stop - mine.start
+        found = jnp.dot(
+            jnp.concatenate(pieces(values), axis=0).astype(BF16), hot[columns],
+            preferred_element_type=F32,
+        )
+        return jnp.sum((found[0:size] + found[size:]) * mask[mine], axis=0, keepdims=True)
+
+    def gather_near(star, expo):
         parts = []
         for at in range(0, star_wide, STAR_ROWS):
             part = star[at : at + STAR_ROWS]
             parts += [part, swap(part)]
         star = jnp.where(lower(star_rows), jnp.concatenate(parts, axis=0), 0.0)
         expo = jnp.where(lower(2 * EXPO_ROWS), 0.0, jnp.concatenate([swap(expo), expo], axis=0))
-        left = jnp.concatenate([star, expo, jnp.zeros((FLAT_ROWS, LANES), F32)], axis=0)
-        right = jnp.concatenate(
-            [jnp.zeros((flat_at, LANES), F32)]
-            + [flat[:, h * LANES : (h + 1) * LANES] for h in range(HALVES)],
-            axis=0,
-        )
-        values = jnp.concatenate([left, right], axis=1)
-        found = jnp.dot(
-            jnp.concatenate(pieces(values), axis=0).astype(BF16), hot[...],
-            preferred_element_type=F32,
-        )
-        return jnp.sum((found[0:rows] + found[rows:]) * mask[...], axis=0, keepdims=True)
-
-    (rhs, count) = scatter(weighted, weights)
+        return find(jnp.concatenate([star, expo], axis=0), near, near_columns)
+
+    def gather_flat(flat):
+        halves = [flat[:, h * LANES : (h + 1) * LANES] for h in range(HALVES)]
+        return find(jnp.concatenate(halves, axis=0), far, far_columns)
+
+    quarter = lax.broadcasted_iota(jnp.int32, (1, LANES), 1) // (LANES // 4)
+
+    def pack(*parts):
+        both = jnp.concatenate(parts, axis=0)
+        both = both + pltpu.roll(both, HALF, 1)
+        both = both + pltpu.roll(both, HALF // 2, 1)
+        row = both[0:1]
+        for k in range(1, len(parts)):
+            row = jnp.where(quarter == k, both[k : k + 1], row)
+        return row
+
+    (rhs, count) = scatter_near(weighted, weights)
     expo0[tile] = jnp.concatenate([rhs[1], count[1]], axis=0)
-    loop0[loop] = jnp.concatenate(
-        [rhs[0], count[0]]
-        + [part[2][:, h * LANES : (h + 1) * LANES] for part in (rhs, count) for h in range(HALVES)],
-        axis=0,
-    )
-    edges0[0:2] = rhs[2][0:2]
-    edges0[2:4] = count[2][0:2]
-    edges0[4:6] = rhs[2][ROWS_DEV - 2 :]
-    edges0[6:8] = count[2][ROWS_DEV - 2 :]
+    loop0[loop] = jnp.concatenate([rhs[0], count[0]], axis=0)
     pl.semaphore_wait(barrier, everyone - 1)
     push_tiles(expo0, 0)
+    push_loops(loop0, 1)
+    (rhs, count) = scatter_flat(weighted, weights)
+    wide0[loop] = jnp.concatenate([rhs, count], axis=0)
+    rhs, count = in_lines(rhs), in_lines(count)
+    edges0[0:2] = rhs[0:2]
+    edges0[2:4] = count[0:2]
+    edges0[4:6] = rhs[ROWS_DEV - 2 :]
+    edges0[6:8] = count[ROWS_DEV - 2 :]
     push_edges(edges0, halo0, 2)
-    push_loops(loop0, 1)
+    push_loops(wide0, 8)
 
     settle(loop0, loops - 1, recv.at[1])
     joint = fold([loop0[l] for l in range(loops)])
     rhs_star = joint[0:star_wide]
     diag_star = joint[star_wide : 2 * star_wide] + RIDGE
-    joint = joint[2 * star_wide :]
-    rhs_mine, count_mine = [
-        jnp.concatenate(
-            [joint[(k * HALVES + h) * ROWS_DEV : (k * HALVES + h + 1) * ROWS_DEV] for h in range(HALVES)],
-            axis=1,
-        )
-        for k in range(2)
-    ]
+    settle(wide0, loops - 1, recv.at[8])
+    joint = fold([wide0[l] for l in range(loops)])
+    rhs_mine = in_lines(joint[0:FLAT_ROWS])
+    count_mine = in_lines(joint[FLAT_ROWS:])
     settle(halo0, 2 * loops, recv.at[2])
     over = fold([halo0[l] for l in range(loops)])
     under = fold([halo0[loops + l] for l in range(loops)])
@@ -261,6 +289,7 @@
     ext[2, whole] = ext[0, whole] / (ext[1, whole] + (4.0 * SMOOTH + RIDGE))
     g_star = rhs_star / diag_star
     g_flat = ext[2, inner]
+    fitted = gather_flat(g_flat)
     settle(expo0, tiles - 1, recv.at[0])
     joint = fold([expo0[t] for t in range(tiles)])
     rhs_expo = joint[0:EXPO_ROWS]
@@ -277,34 +306,37 @@
             lane_fold(own_star * star) + own_expo * lane_fold(expo) + own_flat * lane_fold(flat)
         )
 
-    fitted = gather(g_star, g_expo, g_flat)
+    fitted = fitted + gather_near(g_star, g_expo)
     pulled = weights * fitted
-    ((sum_star, sum_expo, sum_flat),) = scatter(pulled)
-    expo1[tile, 0:EXPO_ROWS] = sum_expo
-    loop1[loop] = jnp.concatenate(
-        [sum_star] + [sum_flat[:, h * LANES : (h + 1) * LANES] for h in range(HALVES)], axis=0
-    )
+    ((sum_star, sum_expo),) = scatter_near(pulled)
+    expo1[tile] = sum_expo
+    loop1[loop] = sum_star
+    push_tiles(expo1, 3)
+    push_loops(loop1, 4)
+    (sum_flat,) = scatter_flat(pulled)
+    wide1[loop] = sum_flat
+    sum_flat = in_lines(sum_flat)
     edges1[0:1] = sum_flat[0:1]
     edges1[1:2] = sum_flat[ROWS_DEV - 1 :]
-    push_tiles(expo1, 3)
     push_edges(edges1, halo1, 5)
-    push_loops(loop1, 4)
+    push_loops(wide1, 9)
     v = ext[2, wide]
     smooth = SMOOTH * (4.0 * v - ext[2, 0 : 2 + ROWS_DEV] - ext[2, 2 : 4 + ROWS_DEV] - beside_columns(v)) + RIDGE * v
     ext[3, wide] = smooth
     smooth_mine = ext[3, inner]
-    dots0[rank, 0:1] = inner_rows(rhs_star * g_star, rhs_expo * g_expo, rhs_mine * g_flat)
-    dots0[rank, 1:2] = lane_fold(pulled * fitted) + inner_rows(
-        RIDGE * g_star * g_star, RIDGE * g_expo * g_expo, smooth_mine * g_flat
+    dots0[rank] = pack(
+        inner_rows(rhs_star * g_star, rhs_expo * g_expo, rhs_mine * g_flat),
+        lane_fold(pulled * fitted) + inner_rows(
+            RIDGE * g_star * g_star, RIDGE * g_expo * g_expo, smooth_mine * g_flat
+        ),
     )
     push_dots(dots0, 6)
 
     settle(loop1, loops - 1, recv.at[4])
     joint = fold([loop1[l] for l in range(loops)])
-    image_star = joint[0:star_wide] + RIDGE * g_star
-    sum_mine = jnp.concatenate(
-        [joint[star_wide + h * ROWS_DEV : star_wide + (h + 1) * ROWS_DEV] for h in range(HALVES)], axis=1
-    )
+    image_star = joint + RIDGE * g_star
+    settle(wide1, loops - 1, recv.at[9])
+    sum_mine = in_lines(fold([wide1[l] for l in range(loops)]))
     settle(halo1, 2 * loops, recv.at[5])
     over = fold([halo1[l] for l in range(loops)])
     under = fold([halo1[loops + l] for l in range(loops)])
@@ -314,21 +346,21 @@
     row = lax.broadcasted_iota(jnp.int32, (2 + ROWS_DEV, FC), 0)
     inside = ((row > 0) | (tile > 0)) & ((row < 1 + ROWS_DEV) | (tile < tiles - 1))
     image_wide = jnp.where(inside, ext[4, wide] + smooth, 0.0)
+    ext[7, wide] = image_wide
+    fitted_image = gather_flat(ext[7, inner] / (count_mine + (4.0 * SMOOTH + RIDGE)))
     settle(expo1, tiles - 1, recv.at[3])
-    joint = fold([expo1[t, 0:EXPO_ROWS] for t in range(tiles)])
+    joint = fold([expo1[t] for t in range(tiles)])
     image_expo = joint + RIDGE * g_expo
 
     def total(buffer, which, count):
         settle(buffer, everyone - 1, recv.at[which])
         joint = fold([buffer[r] for r in range(everyone)])
-        return [jnp.sum(joint[k : k + 1], axis=1, keepdims=True) for k in range(count)]
-
-    ext[7, wide] = image_wide
-    fitted_image = gather(
-        image_star / diag_star,
-        image_expo / diag_expo,
-        ext[7, inner] / (count_mine + (4.0 * SMOOTH + RIDGE)),
-    )
+        return [
+            jnp.sum(jnp.where(quarter == k, joint, 0.0), axis=1, keepdims=True)
+            for k in range(count)
+        ]
+
+    fitted_image = fitted_image + gather_near(image_star / diag_star, image_expo / diag_expo)
     norm, curve = total(dots0, 6, 2)
     alpha = norm / curve
 
@@ -342,12 +374,14 @@
     h_flat = ext[5, inner]
     fitted = fitted - alpha * fitted_image
     beside = ext[5, 1 : 1 + ROWS_DEV] + ext[5, 3 : 3 + ROWS_DEV] + beside_columns(h_flat)
-    dots1[rank, 0:1] = inner_rows(res_star * h_star, res_expo * h_expo, ext[6, inner] * h_flat)
-    dots1[rank, 1:2] = inner_rows(image_star * h_star, image_expo * h_expo, ext[7, inner] * h_flat)
-    dots1[rank, 2:3] = lane_fold(weights * fitted * fitted) + inner_rows(
-        RIDGE * h_star * h_star,
-        RIDGE * h_expo * h_expo,
-        (SMOOTH * (4.0 * h_flat - beside) + RIDGE * h_flat) * h_flat,
+    dots1[rank] = pack(
+        inner_rows(res_star * h_star, res_expo * h_expo, ext[6, inner] * h_flat),
+        inner_rows(image_star * h_star, image_expo * h_expo, ext[7, inner] * h_flat),
+        lane_fold(weights * fitted * fitted) + inner_rows(
+            RIDGE * h_star * h_star,
+            RIDGE * h_expo * h_expo,
+            (SMOOTH * (4.0 * h_flat - beside) + RIDGE * h_flat) * h_flat,
+        ),
     )
     push_dots(dots1, 7)
     norm_next, cross, curve_next = total(dots1, 7, 3)
@@ -367,7 +401,7 @@
     for which, (buffer, count) in enumerate((
         (expo0, tiles - 1), (loop0, loops - 1), (halo0, 2 * loops),
         (expo1, tiles - 1), (loop1, loops - 1), (halo1, 2 * loops),
-        (dots0, everyone - 1), (dots1, everyone - 1),
+        (dots0, everyone - 1), (dots1, everyone - 1), (wide0, loops - 1), (wide1, loops - 1),
     )):
         settle(buffer, count, send.at[which])
 
@@ -397,7 +431,7 @@
     )
     parts = pl.pallas_call(
         functools.partial(kernel, tiles, loops),
-        out_shape=out_shape,
+        out_shape=tuple(pltpu.VMEM(x.shape, x.dtype) for x in out_shape),
         in_specs=[hbm] * 6,
         out_specs=(vmem, vmem, vmem),
         scratch_shapes=[
@@ -411,18 +445,20 @@
             pltpu.VMEM((2 * LANES, seen), BF16),
             pltpu.VMEM((rows, seen), F32),
             pltpu.VMEM((8, FC), F32),
-            pltpu.VMEM((8, FC), F32),
+            pltpu.VMEM((2, FC), F32),
             pltpu.VMEM((8, ROWS_DEV + 8, FC), F32),
-            pltpu.VMEM((loops, 2 * (star_wide + FLAT_ROWS), LANES), F32),
-            pltpu.VMEM((loops, star_wide + FLAT_ROWS, LANES), F32),
+            pltpu.VMEM((loops, 2 * star_wide, LANES), F32),
+            pltpu.VMEM((loops, star_wide, LANES), F32),
+            pltpu.VMEM((loops, 2 * FLAT_ROWS, LANES), F32),
+            pltpu.VMEM((loops, FLAT_ROWS, LANES), F32),
             pltpu.VMEM((tiles, 2 * EXPO_ROWS, LANES), F32),
             pltpu.VMEM((tiles, EXPO_ROWS, LANES), F32),
             pltpu.VMEM((2 * loops, 8, FC), F32),
-            pltpu.VMEM((2 * loops, 8, FC), F32),
-            pltpu.VMEM((tiles * loops, 4, LANES), F32),
-            pltpu.VMEM((tiles * loops, 4, LANES), F32),
-            pltpu.SemaphoreType.DMA((8,)),
-            pltpu.SemaphoreType.DMA((8,)),
+            pltpu.VMEM((2 * loops, 2, FC), F32),
+            pltpu.VMEM((tiles * loops, 1, LANES), F32),
+            pltpu.VMEM((tiles * loops, 1, LANES), F32),
+            pltpu.SemaphoreType.DMA((10,)),
+            pltpu.SemaphoreType.DMA((10,)),
         ],
         compiler_params=pltpu.CompilerParams(
             collective_id=0, has_side_effects=True, vmem_limit_bytes=32 * 1024 * 1024

time: 26.3 us -> 25.3 us (0.962)
  Pallas kernels: 23.6 us -> 22.6 us
    pallas_call x1, Pallas kernels: 22.2 us -> 21.3 us  [on_device(): pl.pallas_call(functools.partial(kernel, tiles, loops), out_shape=tuple((...]
where the time goes in v3:
time: 25.3 us; the launch traced here: 25 us
  Pallas kernels  22.6 us (89%)
  local copies, waits for them, and re-layouts  1.78 us (7%)
  between operations  0.65 us (3%)
    pallas_call x1, Pallas kernels, on_device(): pl.pallas_call(functools.partial(kernel, tiles, loops), out_shape=tuple((...  21.3 us
    unnamed x6, local copies, waits for them, and re-layouts  1.78 us
    pallas_call x1, Pallas kernels, on_device(): pl.pallas_call(write_kernel, out_shape=out_shape, in_specs=[vmem] * 3, ou...  1.34 us

profile of v3, /device:TPU:0, one launch (start us, length us, event | category | flops | bytes accessed | tf_op | source)
XLA Modules:
  0.0 25.0 jit_solution(5821922612211017246)
XLA Ops:
  0.6 21.3 %shard_map.85 = (f32[4,128]{1,0:T(4,128)S(1)}, f32[4,128]{1,0:T(4,128)S(1)}, f32[8,256]{1,0:T(8,128)S(1)}) custom-call(s32[1,16,128]{2,1,0:T(8,128)} %slot_in.1, s32[1,16]{1,0:T(1,128)} %block_in.1, s32[1,16,128]{2,1,0:T(8,128)} %expo_in.1, s32[1,16,128]{2,1,0:T(8,128)} %pixel_in.1, f32[1,16,128]{2,1,0:T(8,128)} %mag_in.1, f32[1,16,128]{2,1,0:T(8,128)} %weight_in.1), custom_call_target="tpu_custom_call" | custom-call | tf_op jit(solution)/shard_map/pallas_call | solution.py:432
  21.9 0.0 copy-start
  21.9 0.6 %copy-done = f32[8,256]{1,0:T(8,128)} copy-done((f32[8,256]{1,0:T(8,128)}, f32[8,256]{1,0:T(8,128)S(1)}, u32[]{:S(2)}) %copy-start) | copy-done | bytes 8216
  22.5 0.0 copy-start.1
  22.5 0.6 %copy-done.1 = f32[4,128]{1,0:T(4,128)} copy-done((f32[4,128]{1,0:T(4,128)}, f32[4,128]{1,0:T(4,128)S(1)}, u32[]{:S(2)}) %copy-start.1) | copy-done | bytes 2072
  23.1 0.0 copy-start.2
  23.1 0.6 %copy-done.2 = f32[4,128]{1,0:T(4,128)} copy-done((f32[4,128]{1,0:T(4,128)}, f32[4,128]{1,0:T(4,128)S(1)}, u32[]{:S(2)}) %copy-start.2) | copy-done | bytes 2072
  23.7 1.3 %shard_map.86 = (f32[4,128]{1,0:T(4,128)}, f32[4,128]{1,0:T(4,128)}, f32[8,256]{1,0:T(8,128)}) custom-call(f32[4,128]{1,0:T(4,128)} %copy-done.1, f32[4,128]{1,0:T(4,128)} %copy-done.2, f32[8,256]{1,0:T(8,128)} %copy-done), custom_call_target="tpu_custom_call" | custom-call | tf_op jit(solution)/shard_map/pallas_call | solution.py:470
Async XLA Ops:
  21.9 0.6 %copy-start = (f32[8,256]{1,0:T(8,128)}, f32[8,256]{1,0:T(8,128)S(1)}, u32[]{:S(2)}) copy-start(f32[8,256]{1,0:T(8,128)S(1)} %get-tuple-element.11.flat) | copy-start | bytes 24580
  22.5 0.6 %copy-start.1 = (f32[4,128]{1,0:T(4,128)}, f32[4,128]{1,0:T(4,128)S(1)}, u32[]{:S(2)}) copy-start(f32[4,128]{1,0:T(4,128)S(1)} %get-tuple-element.9.star) | copy-start | bytes 6148
  23.1 0.6 %copy-start.2 = (f32[4,128]{1,0:T(4,128)}, f32[4,128]{1,0:T(4,128)S(1)}, u32[]{:S(2)}) copy-start(f32[4,128]{1,0:T(4,128)S(1)} %get-tuple-element.10.expo) | copy-start | bytes 6148

commit v4 on v3

--- a/solution.py
+++ b/solution.py
@@ -154,18 +154,14 @@
         at = slice(b * LANES, (b + 1) * LANES)
         star = block_ref[0, b] * STAR_BLK + slot_ref[0, b : b + 1, :]
         expo = expo_ref[0, b : b + 1, :]
-        pixel = pixel_ref[0, b : b + 1, :]
         hot[0:HALF, at] = jnp.where(half_ids == (star & (HALF - 1)), 1.0, 0.0).astype(BF16)
         hot[HALF:LANES, at] = jnp.where(half_ids == (expo & (HALF - 1)), 1.0, 0.0).astype(BF16)
-        hot[LANES : 2 * LANES, at] = jnp.where(lane_ids == (pixel & (LANES - 1)), 1.0, 0.0).astype(BF16)
         star_high = (
             (b // per_shard) * (2 * STAR_ROWS) + ((star // HALF) & 1) * STAR_ROWS + star // LANES
         )
         expo_high = ((expo // HALF) & 1) * EXPO_ROWS + expo // LANES
-        pixel_high = (pixel // LANES) % HALVES * ROWS_DEV + pixel // FC
         mask[0:star_rows, at] = jnp.where(star_ids == star_high, 1.0, 0.0)
         mask[expo_at:flat_at, at] = jnp.where(expo_ids == expo_high, 1.0, 0.0)
-        mask[flat_at:rows, at] = jnp.where(flat_ids == pixel_high, 1.0, 0.0)
 
     weights = line(weight_ref[0])
     weighted = weights * line(mag_ref[0])
@@ -254,6 +250,12 @@
     pl.semaphore_wait(barrier, everyone - 1)
     push_tiles(expo0, 0)
     push_loops(loop0, 1)
+    for b in range(blocks):
+        at = slice(b * LANES, (b + 1) * LANES)
+        pixel = pixel_ref[0, b : b + 1, :]
+        hot[LANES : 2 * LANES, at] = jnp.where(lane_ids == (pixel & (LANES - 1)), 1.0, 0.0).astype(BF16)
+        pixel_high = (pixel // LANES) % HALVES * ROWS_DEV + pixel // FC
+        mask[flat_at:rows, at] = jnp.where(flat_ids == pixel_high, 1.0, 0.0)
     (rhs, count) = scatter_flat(weighted, weights)
     wide0[loop] = jnp.concatenate([rhs, count], axis=0)
     rhs, count = in_lines(rhs), in_lines(count)
@@ -290,26 +292,36 @@
     g_star = rhs_star / diag_star
     g_flat = ext[2, inner]
     fitted = gather_flat(g_flat)
+    shard_row = lax.broadcasted_iota(jnp.int32, (star_wide, LANES), 0) // STAR_ROWS
+    own_star = jnp.where(shard_row == loop, 1.0, 0.0)
+    own_expo = jnp.where(tile == 0, 1.0, 0.0)
+    own_flat = jnp.where(loop == 0, 1.0, 0.0)
+
+    def inner_rows(star, expo, flat):
+        return (
+            lane_fold(own_star * star) + own_expo * lane_fold(expo) + own_flat * lane_fold(flat)
+        )
+
+    v = ext[2, wide]
+    smooth = SMOOTH * (4.0 * v - ext[2, 0 : 2 + ROWS_DEV] - ext[2, 2 : 4 + ROWS_DEV] - beside_columns(v)) + RIDGE * v
+    ext[3, wide] = smooth
+    smooth_mine = ext[3, inner]
+    norm = lane_fold(own_star * rhs_star * g_star) + own_flat * lane_fold(rhs_mine * g_flat)
+    curve = RIDGE * lane_fold(own_star * g_star * g_star) + own_flat * lane_fold(smooth_mine * g_flat)
     settle(expo0, tiles - 1, recv.at[0])
     joint = fold([expo0[t] for t in range(tiles)])
     rhs_expo = joint[0:EXPO_ROWS]
     diag_expo = joint[EXPO_ROWS:] + RIDGE
     g_expo = rhs_expo / diag_expo
 
-    shard_row = lax.broadcasted_iota(jnp.int32, (star_wide, LANES), 0) // STAR_ROWS
-    own_star = jnp.where(shard_row == loop, 1.0, 0.0)
-    own_expo = jnp.where(tile == 0, 1.0, 0.0)
-    own_flat = jnp.where(loop == 0, 1.0, 0.0)
-
-    def inner_rows(star, expo, flat):
-        return (
-            lane_fold(own_star * star) + own_expo * lane_fold(expo) + own_flat * lane_fold(flat)
-        )
-
     fitted = fitted + gather_near(g_star, g_expo)
     pulled = weights * fitted
     ((sum_star, sum_expo),) = scatter_near(pulled)
-    expo1[tile] = sum_expo
+    expo1[tile, 0:EXPO_ROWS] = sum_expo
+    expo1[tile, EXPO_ROWS : EXPO_ROWS + 1] = pack(
+        norm + own_expo * lane_fold(rhs_expo * g_expo),
+        curve + lane_fold(pulled * fitted) + (own_expo * RIDGE) * lane_fold(g_expo * g_expo),
+    )
     loop1[loop] = sum_star
     push_tiles(expo1, 3)
     push_loops(loop1, 4)
@@ -320,17 +332,6 @@
     edges1[1:2] = sum_flat[ROWS_DEV - 1 :]
     push_edges(edges1, halo1, 5)
     push_loops(wide1, 9)
-    v = ext[2, wide]
-    smooth = SMOOTH * (4.0 * v - ext[2, 0 : 2 + ROWS_DEV] - ext[2, 2 : 4 + ROWS_DEV] - beside_columns(v)) + RIDGE * v
-    ext[3, wide] = smooth
-    smooth_mine = ext[3, inner]
-    dots0[rank] = pack(
-        inner_rows(rhs_star * g_star, rhs_expo * g_expo, rhs_mine * g_flat),
-        lane_fold(pulled * fitted) + inner_rows(
-            RIDGE * g_star * g_star, RIDGE * g_expo * g_expo, smooth_mine * g_flat
-        ),
-    )
-    push_dots(dots0, 6)
 
     settle(loop1, loops - 1, recv.at[4])
     joint = fold([loop1[l] for l in range(loops)])
@@ -350,18 +351,20 @@
     fitted_image = gather_flat(ext[7, inner] / (count_mine + (4.0 * SMOOTH + RIDGE)))
     settle(expo1, tiles - 1, recv.at[3])
     joint = fold([expo1[t] for t in range(tiles)])
-    image_expo = joint + RIDGE * g_expo
-
-    def total(buffer, which, count):
-        settle(buffer, everyone - 1, recv.at[which])
-        joint = fold([buffer[r] for r in range(everyone)])
+    dots0[loop] = joint[EXPO_ROWS:]
+    push_loops(dots0, 6)
+    image_expo = joint[0:EXPO_ROWS] + RIDGE * g_expo
+
+    def total(buffer, which, size, count):
+        settle(buffer, size - 1, recv.at[which])
+        joint = fold([buffer[r] for r in range(size)])
         return [
             jnp.sum(jnp.where(quarter == k, joint, 0.0), axis=1, keepdims=True)
             for k in range(count)
         ]
 
     fitted_image = fitted_image + gather_near(image_star / diag_star, image_expo / diag_expo)
-    norm, curve = total(dots0, 6, 2)
+    norm, curve = total(dots0, 6, loops, 2)
     alpha = norm / curve
 
     res_star = rhs_star - alpha * image_star
@@ -384,7 +387,7 @@
         ),
     )
     push_dots(dots1, 7)
-    norm_next, cross, curve_next = total(dots1, 7, 3)
+    norm_next, cross, curve_next = total(dots1, 7, everyone, 3)
     ratio = norm_next / norm
     step = norm_next / (curve_next + ratio * (2.0 * cross + ratio * curve))
 
@@ -401,7 +404,7 @@
     for which, (buffer, count) in enumerate((
         (expo0, tiles - 1), (loop0, loops - 1), (halo0, 2 * loops),
         (expo1, tiles - 1), (loop1, loops - 1), (halo1, 2 * loops),
-        (dots0, everyone - 1), (dots1, everyone - 1), (wide0, loops - 1), (wide1, loops - 1),
+        (dots0, loops - 1), (dots1, everyone - 1), (wide0, loops - 1), (wide1, loops - 1),
     )):
         settle(buffer, count, send.at[which])
 
@@ -452,10 +455,10 @@
             pltpu.VMEM((loops, 2 * FLAT_ROWS, LANES), F32),
             pltpu.VMEM((loops, FLAT_ROWS, LANES), F32),
             pltpu.VMEM((tiles, 2 * EXPO_ROWS, LANES), F32),
-            pltpu.VMEM((tiles, EXPO_ROWS, LANES), F32),
+            pltpu.VMEM((tiles, EXPO_ROWS + 1, LANES), F32),
             pltpu.VMEM((2 * loops, 8, FC), F32),
             pltpu.VMEM((2 * loops, 2, FC), F32),
-            pltpu.VMEM((tiles * loops, 1, LANES), F32),
+            pltpu.VMEM((loops, 1, LANES), F32),
             pltpu.VMEM((tiles * loops, 1, LANES), F32),
             pltpu.SemaphoreType.DMA((10,)),
             pltpu.SemaphoreType.DMA((10,)),
@@ -473,6 +476,7 @@
         in_specs=[vmem] * 3,
         out_specs=(hbm,) * 3,
         scratch_shapes=[pltpu.SemaphoreType.DMA((3,))],
+        compiler_params=pltpu.CompilerParams(vmem_limit_bytes=1024 * 1024),
     )(*parts)
     return star.reshape(-1), expo.reshape(-1), flat
 

time: 25.3 us -> 24.6 us (0.972)
  local copies, waits for them, and re-layouts: 1.78 us -> 0 us
  Pallas kernels: 22.6 us -> 23.7 us
    pallas_call x1, Pallas kernels: 21.3 us -> 23.1 us  [on_device(): pl.pallas_call(functools.partial(kernel, tiles, loops), out_shape=tuple((...]
    unnamed x6 -> x0, local copies, waits for them, and re-layouts: 1.78 us -> none
    pallas_call x1, Pallas kernels: 1.34 us -> 0.64 us  [on_device(): pl.pallas_call(write_kernel, out_shape=out_shape, in_specs=[vmem] * 3, ou...]
where the time goes in v4:
time: 24.6 us; the launch traced here: 24.4 us
  Pallas kernels  23.7 us (96%)
  between operations  0.64 us (3%)
    pallas_call x1, Pallas kernels, on_device(): pl.pallas_call(functools.partial(kernel, tiles, loops), out_shape=tuple((...  23.1 us
    pallas_call x1, Pallas kernels, on_device(): pl.pallas_call(write_kernel, out_shape=out_shape, in_specs=[vmem] * 3, ou...  0.64 us

profile of v4, /device:TPU:0, one launch (start us, length us, event | category | flops | bytes accessed | tf_op | source)
XLA Modules:
  0.0 24.4 jit_solution(5075747474875656093)
XLA Ops:
  0.6 23.1 %shard_map.85 = (f32[4,128]{1,0:T(4,128)S(1)}, f32[4,128]{1,0:T(4,128)S(1)}, f32[8,256]{1,0:T(8,128)S(1)}) custom-call(s32[1,16,128]{2,1,0:T(8,128)} %slot_in.1, s32[1,16]{1,0:T(1,128)} %block_in.1, s32[1,16,128]{2,1,0:T(8,128)} %expo_in.1, s32[1,16,128]{2,1,0:T(8,128)} %pixel_in.1, f32[1,16,128]{2,1,0:T(8,128)} %mag_in.1, f32[1,16,128]{2,1,0:T(8,128)} %weight_in.1), custom_call_target="tpu_custom_call" | custom-call | tf_op jit(solution)/shard_map/pallas_call | solution.py:435
  23.7 0.6 %shard_map.86 = (f32[4,128]{1,0:T(4,128)}, f32[4,128]{1,0:T(4,128)}, f32[8,256]{1,0:T(8,128)}) custom-call(f32[4,128]{1,0:T(4,128)S(1)} %get-tuple-element.9.star, f32[4,128]{1,0:T(4,128)S(1)} %get-tuple-element.10.expo, f32[8,256]{1,0:T(8,128)S(1)} %get-tuple-element.11.flat), custom_call_target="tpu_custom_call" | custom-call | tf_op jit(solution)/shard_map/pallas_call | solution.py:473

commit v5 on v3

--- a/solution.py
+++ b/solution.py
@@ -473,6 +473,7 @@
         in_specs=[vmem] * 3,
         out_specs=(hbm,) * 3,
         scratch_shapes=[pltpu.SemaphoreType.DMA((3,))],
+        compiler_params=pltpu.CompilerParams(vmem_limit_bytes=1024 * 1024),
     )(*parts)
     return star.reshape(-1), expo.reshape(-1), flat
 

time: 25.3 us -> 22.8 us (0.901)
  local copies, waits for them, and re-layouts: 1.78 us -> 0 us
  Pallas kernels: 22.6 us -> 21.9 us
    unnamed x6 -> x0, local copies, waits for them, and re-layouts: 1.78 us -> none
    pallas_call x1, Pallas kernels: 1.34 us -> 0.64 us  [on_device(): pl.pallas_call(write_kernel, out_shape=out_shape, in_specs=[vmem] * 3, ou...]
where the time goes in v5:
time: 22.8 us; the launch traced here: 22.6 us
  Pallas kernels  21.9 us (96%)
  between operations  0.64 us (3%)
    pallas_call x1, Pallas kernels, on_device(): pl.pallas_call(functools.partial(kernel, tiles, loops), out_shape=tuple((...  21.3 us
    pallas_call x1, Pallas kernels, on_device(): pl.pallas_call(write_kernel, out_shape=out_shape, in_specs=[vmem] * 3, ou...  0.64 us

profile of v5, /device:TPU:0, one launch (start us, length us, event | category | flops | bytes accessed | tf_op | source)
XLA Modules:
  0.0 22.6 jit_solution(14718473299906403352)
XLA Ops:
  0.6 21.3 %shard_map.85 = (f32[4,128]{1,0:T(4,128)S(1)}, f32[4,128]{1,0:T(4,128)S(1)}, f32[8,256]{1,0:T(8,128)S(1)}) custom-call(s32[1,16,128]{2,1,0:T(8,128)} %slot_in.1, s32[1,16]{1,0:T(1,128)} %block_in.1, s32[1,16,128]{2,1,0:T(8,128)} %expo_in.1, s32[1,16,128]{2,1,0:T(8,128)} %pixel_in.1, f32[1,16,128]{2,1,0:T(8,128)} %mag_in.1, f32[1,16,128]{2,1,0:T(8,128)} %weight_in.1), custom_call_target="tpu_custom_call" | custom-call | tf_op jit(solution)/shard_map/pallas_call | solution.py:432
  21.9 0.6 %shard_map.86 = (f32[4,128]{1,0:T(4,128)}, f32[4,128]{1,0:T(4,128)}, f32[8,256]{1,0:T(8,128)}) custom-call(f32[4,128]{1,0:T(4,128)S(1)} %get-tuple-element.9.star, f32[4,128]{1,0:T(4,128)S(1)} %get-tuple-element.10.expo, f32[8,256]{1,0:T(8,128)S(1)} %get-tuple-element.11.flat), custom_call_target="tpu_custom_call" | custom-call | tf_op jit(solution)/shard_map/pallas_call | solution.py:470
